TPU v7x, 32 devices: a whole 2x2x4 slice. The times are simulated.
32 devices in a mesh: dp: 8 (over z, y), tensor: 4 (over x, core).
Axes of the slice: x: 2, y: 2, z: 4, core: 2. Of those that a mesh axis runs over, the one named last changes fastest.
Arguments:
- tokens: bfloat16 [24, 4, 128, 1024], P(None, 'tensor', 'dp'), may hold values from -6 to 6
- cotangent: bfloat16 [24, 4, 128, 1024], P(None, 'tensor', 'dp'), may hold values from -6 to 6
- lengths: int32 [24], replicated, may hold values from 1 to 512, 10752 in all
- order: int32 [24], replicated, may hold values from 0 to 23, each once
- triple_weight: bfloat16 [3, 1024, 1024], P(None, 'dp', 'tensor'), may hold values from -0.1875 to 0.1875
- output_weight: bfloat16 [1024, 1024], P(None, 'dp'), may hold values from -2 to 2
- expand_weight: bfloat16 [1024, 4096], P('dp', 'tensor'), may hold values from -0.1875 to 0.1875
- shrink_weight: bfloat16 [4096, 1024], P('tensor', 'dp'), may hold values from -0.09375 to 0.09375
- biases: bfloat16 [6, 1024], P(None, 'dp'), may hold values from -3 to 3
- gains: bfloat16 [2, 1024], P(None, 'dp'), may hold values from 0.25 to 1.75
- expand_bias: bfloat16 [4096], P('dp'), may hold values from -3 to 3
Outputs:
- mixed: bfloat16 [24, 4, 128, 1024], P(None, 'tensor', 'dp')
- input_grad: bfloat16 [24, 4, 128, 1024], P(None, 'tensor', 'dp')
- triple_grad: float32 [3, 1024, 1024], P(None, 'dp', 'tensor')
- output_grad: float32 [1024, 1024], P('tensor', 'dp')
- expand_grad: float32 [1024, 4096], P('dp', 'tensor')
- shrink_grad: float32 [4096, 1024], P('tensor', 'dp')
- biases_grad: float32 [6, 1024], P(None, 'dp')
- gains_grad: float32 [2, 1024], P(None, 'dp')
- expand_bias_grad: float32 [4096], P('dp')
Inputs may be any that keep to these rules, and one draw needn't show every extreme that they name: lengths[i] counts the valid leading positions of sequence i; the longest is exactly 512. `order`: a permutation of the sequence numbers.
All inputs are finite; a program needn't handle non-finite values.
Results may differ from a plain program's by a relative error of at most 0.02.
Values may be sent and summed in bfloat16 or wider, within the bound.
A program may use at most 128 MiB of HBM per device.

v0:
```python
import math

import jax
import jax.numpy as jnp
from jax import lax
from jax.sharding import PartitionSpec as P

HEAD_DIM = 64


EPSILON = 1e-12
MASKED = -1e30


def normalize(values, gain, shift):
    center = values - jnp.mean(values, axis=-1, keepdims=True)
    spread = jnp.mean(center * center, axis=-1, keepdims=True)
    inv_std = lax.rsqrt(spread + EPSILON)
    scaled = center * inv_std
    return (scaled * gain + shift, scaled, inv_std)


def normalize_back(grad_rows, scaled, inv_std, gain):
    pushed = grad_rows * gain
    first = jnp.mean(pushed, axis=-1, keepdims=True)
    second = jnp.mean(pushed * scaled, axis=-1, keepdims=True)
    return inv_std * (pushed - first - scaled * second)


def gelu_exact(values):
    return 0.5 * values * (1.0 + jax.scipy.special.erf(values / math.sqrt(2.0)))


def gelu_slope(values):
    return 0.5 * (1.0 + jax.scipy.special.erf(values / math.sqrt(2.0))) + values * jnp.exp(
        -0.5 * values * values
    ) / math.sqrt(2.0 * math.pi)


def split_heads(rows):
    return rows.reshape(rows.shape[0], rows.shape[1] // HEAD_DIM, HEAD_DIM)


def score_block(queries, key_rows, seq_length):
    raw_scores = jnp.einsum("qhe,khe->hqk", queries, key_rows, preferred_element_type=jnp.float32)
    scores = raw_scores * (1.0 / math.sqrt(HEAD_DIM))
    visible = jnp.arange(key_rows.shape[0]) < seq_length
    return jnp.where(visible[None, None, :], scores, MASKED)


def attend(seq_item):
    queries, key_rows, value_rows, seq_length = seq_item
    queries = split_heads(queries)
    key_rows = split_heads(key_rows)
    value_rows = split_heads(value_rows)
    masked = score_block(queries, key_rows, seq_length)
    highest = jnp.max(masked, axis=-1, keepdims=True)
    totals = jnp.sum(jnp.exp(masked - highest), axis=-1, keepdims=True)
    log_totals = highest + jnp.log(totals)
    probs = jnp.exp(masked - log_totals).astype(jnp.bfloat16)
    blended = jnp.einsum("hqk,khe->qhe", probs, value_rows, preferred_element_type=jnp.float32)
    return (blended.astype(jnp.bfloat16).reshape(queries.shape[0], -1), log_totals[..., 0])


def attend_back(seq_item):
    queries, key_rows, value_rows, grad_rows, log_totals, seq_length = seq_item
    queries = split_heads(queries)
    key_rows = split_heads(key_rows)
    value_rows = split_heads(value_rows)
    grad_heads = split_heads(grad_rows)
    masked = score_block(queries, key_rows, seq_length)
    probs = jnp.exp(masked - log_totals[..., None])
    grad_probs = jnp.einsum(
        "qhe,khe->hqk", grad_heads, value_rows, preferred_element_type=jnp.float32
    )
    inner = jnp.sum(probs * grad_probs, axis=-1, keepdims=True)
    grad_scores = (probs * (grad_probs - inner)).astype(jnp.bfloat16)
    score_scale = 1.0 / math.sqrt(HEAD_DIM)
    grad_query = (
        jnp.einsum("hqk,khe->qhe", grad_scores, key_rows, preferred_element_type=jnp.float32)
        * score_scale
    )
    grad_key = (
        jnp.einsum("hqk,qhe->khe", grad_scores, queries, preferred_element_type=jnp.float32)
        * score_scale
    )
    grad_value = jnp.einsum(
        "hqk,qhe->khe", probs.astype(jnp.bfloat16), grad_heads, preferred_element_type=jnp.float32
    )
    row_count = queries.shape[0]
    return (
        grad_query.astype(jnp.bfloat16).reshape(row_count, -1),
        grad_key.astype(jnp.bfloat16).reshape(row_count, -1),
        grad_value.astype(jnp.bfloat16).reshape(row_count, -1),
    )


def body(
    tokens,
    cotangent,
    lengths,
    order,
    triple_weight,
    output_weight,
    expand_weight,
    shrink_weight,
    biases,
    gains,
    expand_bias,
):
    seq_count = order.shape[0]
    per_group = seq_count // lax.axis_size("dp")
    tensor_size = lax.axis_size("tensor")
    member = lax.axis_index("dp")
    my_rank = lax.axis_index("tensor")
    slot_ids = jnp.arange(seq_count, dtype=jnp.int32)
    inverse = jnp.zeros((seq_count,), jnp.int32).at[order].set(slot_ids)
    local_x, local_dy = (
        lax.all_to_all(tokens[inverse], "dp", split_axis=0, concat_axis=2, tiled=True),
        lax.all_to_all(cotangent, "dp", split_axis=0, concat_axis=2, tiled=True),
    )
    quarter = local_x.shape[2]
    model_width = local_x.shape[3]
    full_length = quarter * tensor_size
    my_lengths = lax.dynamic_slice_in_dim(lengths, member * per_group, per_group)
    gathered = (
        lax.all_gather(triple_weight, "dp", axis=1, tiled=True),
        lax.all_gather(output_weight, "dp", axis=1, tiled=True),
        lax.all_gather(expand_weight, "dp", axis=0, tiled=True),
        lax.all_gather(shrink_weight, "dp", axis=1, tiled=True),
        lax.all_gather(biases, "dp", axis=1, tiled=True),
        lax.all_gather(gains, "dp", axis=1, tiled=True),
        lax.all_gather(expand_bias, "dp", axis=0, tiled=True),
    )
    query_key_value_proj, out_weight, widen_projection, shrink, bias_rows, gain_rows, exp_bias = (
        gathered
    )
    head_width = query_key_value_proj.shape[2]
    hidden_width = widen_projection.shape[1]
    out_heads = lax.dynamic_slice_in_dim(out_weight, my_rank * head_width, head_width, 0)
    bias_query = lax.dynamic_slice_in_dim(bias_rows[0], my_rank * head_width, head_width).astype(
        jnp.float32
    )
    bias_value = lax.dynamic_slice_in_dim(bias_rows[1], my_rank * head_width, head_width).astype(
        jnp.float32
    )
    bias_hidden = lax.dynamic_slice_in_dim(exp_bias, my_rank * hidden_width, hidden_width).astype(
        jnp.float32
    )
    bias_stack = jnp.stack([bias_query, jnp.zeros_like(bias_query), bias_value])
    gain_first = gain_rows[0].astype(jnp.float32)
    gain_second = gain_rows[1].astype(jnp.float32)
    full_shape = (per_group, tensor_size, quarter, model_width)
    token_all_rows = lax.all_gather(local_x, "tensor", axis=1, tiled=True).reshape(
        per_group, full_length, model_width
    )
    projected = (
        jnp.einsum(
            "jah,rhu->rjau",
            token_all_rows,
            query_key_value_proj,
            preferred_element_type=jnp.float32,
        )
        + bias_stack[:, None, None, :]
    ).astype(jnp.bfloat16)
    attended, log_totals = lax.map(attend, (projected[0], projected[1], projected[2], my_lengths))
    attn_terms = jnp.einsum(
        "sle,em->slm", attended, out_heads, preferred_element_type=jnp.float32
    ).reshape(full_shape)
    attn_sum = lax.psum_scatter(attn_terms, "tensor", scatter_dimension=1, tiled=True)
    hidden_in = local_x.astype(jnp.float32) + (attn_sum + bias_rows[2].astype(jnp.float32))
    normed, normed_scaled, normed_inv = normalize(
        hidden_in, gain_first, bias_rows[3].astype(jnp.float32)
    )
    normalized_all_rows = lax.all_gather(
        normed.astype(jnp.bfloat16), "tensor", axis=1, tiled=True
    ).reshape(per_group, full_length, model_width)
    pre_act = (
        jnp.einsum(
            "uqj,jt->uqt", normalized_all_rows, widen_projection, preferred_element_type=jnp.float32
        )
        + bias_hidden
    )
    hidden = gelu_exact(pre_act).astype(jnp.bfloat16)
    ffn_terms = jnp.einsum(
        "slf,fm->slm", hidden, shrink, preferred_element_type=jnp.float32
    ).reshape(full_shape)
    ffn_sum = lax.psum_scatter(
        ffn_terms.astype(jnp.bfloat16), "tensor", scatter_dimension=1, tiled=True
    ).astype(jnp.float32)
    total_rows = normed + (ffn_sum + bias_rows[4].astype(jnp.float32))
    output, out_scaled, out_inv = normalize(
        total_rows, gain_second, bias_rows[5].astype(jnp.float32)
    )
    positions = my_rank * quarter + jnp.arange(quarter)
    valid = (positions[None, :] < my_lengths[:, None]).astype(jnp.float32)
    grad_out = local_dy.astype(jnp.float32) * valid[:, None, :, None]
    row_axes = (0, 1, 2)
    gain_grad_second = jnp.sum(grad_out * out_scaled, axis=row_axes)
    shift_grad_second = jnp.sum(grad_out, axis=row_axes)
    grad_total = normalize_back(grad_out, out_scaled, out_inv, gain_second)
    branch_bias_grad = jnp.sum(grad_total, axis=row_axes)
    grad_branch = lax.all_gather(
        grad_total.astype(jnp.bfloat16), "tensor", axis=1, tiled=True
    ).reshape(per_group, full_length, model_width)
    shrink_grad = jnp.einsum("slf,slm->fm", hidden, grad_branch, preferred_element_type=jnp.float32)
    grad_hidden = jnp.einsum("slm,fm->slf", grad_branch, shrink, preferred_element_type=jnp.float32)
    preactivation_grad = (grad_hidden * gelu_slope(pre_act)).astype(jnp.bfloat16)
    hidden_bias_grad = jnp.sum(preactivation_grad, axis=(0, 1), dtype=jnp.float32)
    expand_grad = jnp.einsum(
        "mgc,mga->ca", normalized_all_rows, preactivation_grad, preferred_element_type=jnp.float32
    )
    normed_terms = jnp.einsum(
        "cpk,rk->cpr", preactivation_grad, widen_projection, preferred_element_type=jnp.float32
    ).reshape(full_shape)
    grad_normed = grad_total + lax.psum_scatter(
        normed_terms.astype(jnp.bfloat16), "tensor", scatter_dimension=1, tiled=True
    ).astype(jnp.float32)
    first_norm_gain_grad = jnp.sum(grad_normed * normed_scaled, axis=row_axes)
    shift_grad_first = jnp.sum(grad_normed, axis=row_axes)
    grad_hidden_in = normalize_back(grad_normed, normed_scaled, normed_inv, gain_first)
    out_bias_grad = jnp.sum(grad_hidden_in, axis=row_axes)
    grad_attn = lax.all_gather(
        grad_hidden_in.astype(jnp.bfloat16), "tensor", axis=1, tiled=True
    ).reshape(per_group, full_length, model_width)
    output_grad = jnp.einsum("sle,slm->em", attended, grad_attn, preferred_element_type=jnp.float32)
    grad_blended = jnp.einsum(
        "slm,em->sle", grad_attn, out_heads, preferred_element_type=jnp.float32
    ).astype(jnp.bfloat16)
    grad_query, grad_key, grad_value = lax.map(
        attend_back,
        (projected[0], projected[1], projected[2], grad_blended, log_totals, my_lengths),
    )
    projection_output_grad = jnp.stack([grad_query, grad_key, grad_value])
    query_bias_grad = jnp.sum(grad_query, axis=(0, 1), dtype=jnp.float32)
    value_bias_grad = jnp.sum(grad_value, axis=(0, 1), dtype=jnp.float32)
    triple_grad = jnp.einsum(
        "xyt,vxyu->vtu", token_all_rows, projection_output_grad, preferred_element_type=jnp.float32
    )
    token_terms = jnp.einsum(
        "atpi,aki->tpk",
        projection_output_grad,
        query_key_value_proj,
        preferred_element_type=jnp.float32,
    ).reshape(full_shape)
    grad_tokens = grad_hidden_in + lax.psum_scatter(
        token_terms.astype(jnp.bfloat16), "tensor", scatter_dimension=1, tiled=True
    ).astype(jnp.float32)
    zero_row = jnp.zeros((model_width,), jnp.float32)
    query_full = lax.dynamic_update_slice_in_dim(zero_row, query_bias_grad, my_rank * head_width, 0)
    value_full = lax.dynamic_update_slice_in_dim(zero_row, value_bias_grad, my_rank * head_width, 0)
    bias_grad = jnp.stack(
        [
            query_full,
            value_full,
            out_bias_grad,
            shift_grad_first,
            branch_bias_grad,
            shift_grad_second,
        ]
    )
    gain_grad = jnp.stack([first_norm_gain_grad, gain_grad_second])
    hidden_full = lax.dynamic_update_slice_in_dim(
        jnp.zeros((exp_bias.shape[0],), jnp.float32), hidden_bias_grad, my_rank * hidden_width, 0
    )
    bias_grad, gain_grad, hidden_full = (
        lax.psum(bias_grad.astype(jnp.bfloat16), "tensor").astype(jnp.float32),
        lax.psum(gain_grad.astype(jnp.bfloat16), "tensor").astype(jnp.float32),
        lax.psum(hidden_full.astype(jnp.bfloat16), "tensor").astype(jnp.float32),
    )
    shards = (
        lax.psum_scatter(triple_grad, "dp", scatter_dimension=1, tiled=True),
        lax.psum_scatter(output_grad, "dp", scatter_dimension=1, tiled=True),
        lax.psum_scatter(expand_grad, "dp", scatter_dimension=0, tiled=True),
        lax.psum_scatter(shrink_grad, "dp", scatter_dimension=1, tiled=True),
        lax.psum_scatter(bias_grad, "dp", scatter_dimension=1, tiled=True),
        lax.psum_scatter(gain_grad, "dp", scatter_dimension=1, tiled=True),
        lax.psum_scatter(hidden_full, "dp", scatter_dimension=0, tiled=True),
    )
    mixed_rows, back_rows = (
        lax.all_to_all(output.astype(jnp.bfloat16), "dp", split_axis=2, concat_axis=0, tiled=True),
        lax.all_to_all(
            grad_tokens.astype(jnp.bfloat16), "dp", split_axis=2, concat_axis=0, tiled=True
        ),
    )
    return (
        mixed_rows,
        back_rows[order],
        shards[0],
        shards[1],
        shards[2],
        shards[3],
        shards[4],
        shards[5],
        shards[6],
    )


def solution(mesh):
    return jax.shard_map(
        body,
        mesh=mesh,
        in_specs=(
            P(None, "tensor", "dp", None),
            P(None, "tensor", "dp", None),
            P(),
            P(),
            P(None, "dp", "tensor"),
            P(None, "dp"),
            P("dp", "tensor"),
            P("tensor", "dp"),
            P(None, "dp"),
            P(None, "dp"),
            P("dp"),
        ),
        out_specs=(
            P(None, "tensor", "dp", None),
            P(None, "tensor", "dp", None),
            P(None, "dp", "tensor"),
            P("tensor", "dp"),
            P("dp", "tensor"),
            P("tensor", "dp"),
            P(None, "dp"),
            P(None, "dp"),
            P("dp"),
        ),
        check_vma=False,
    )
```

profile of v0, /device:TPU:0, one launch (start us, length us, event | category | flops | bytes accessed | tf_op | source)
XLA Modules:
  0.0 1087.0 jit_solution(4331400112678534278)
XLA Ops:
  9.3 27.2 %all_to_all.63 = bf16[24,1,16,1024]{3,2,1,0:T(8,128)(2,1)S(1)} all-to-all(bf16[24,1,16,1024]{3,2,1,0:T(8,128)(2,1)S(1)} %bitcast.249), channel_id=1, replica_groups=mesh['dp'=8,'tensor'=4] {'dp'}, dimensions={0} | all-to-all | bytes 1572864 | tf_op jit(solution)/shard_map/all_to_all | solution.py:119
  39.1 26.0 %all_gather.35 = bf16[6,1024]{1,0:T(8,128)(2,1)S(1)} all-gather(bf16[6,128]{1,0:T(8,128)(2,1)S(1)} %copy-done.19), channel_id=1, replica_groups=mesh['dp'=8,'tensor'=4] {'dp'}, dimensions={1}, use_global_device_ids=true | all-gather | bytes 13824 | tf_op jit(solution)/shard_map/all_gather | solution.py:131
  67.5 44.1 %all-gather.12.cloned.1.call-done = bf16[3,1024,256]{2,1,0:T(8,128)(2,1)} async-done(((bf16[3,128,256]{2,1,0:T(8,128)(2,1)}), bf16[3,1024,256]{2,1,0:T(8,128)(2,1)}) %all-gather.12.cloned.1.call-update) | async-done | bytes 1572880 | tf_op jit(solution)/shard_map/all_gather | solution.py:127
  117.8 15.3 %while.26 = (s32[]{:T(128)}, bf16[3,512,256]{1,2,0:T(8,128)(2,1)}, f32[3,4,512]{2,1,0:T(4,128)S(1)}, bf16[3,512,256]{1,2,0:T(8,128)(2,1)S(1)}, s32[3]{0:T(128)S(...) while((s32[]{:T(128)}, bf16[3,512,256]{1,2,0:T(8,128)(2,1)}, ...), condition=%wide.region_4.5_spmd, body=%wide.region_1.4_spmd.sunk | while | flops 280099328 | bytes 15796349 | solution.py:166
  133.1 30.5 %all-gather.14.cloned.1.call-done = bf16[1024,1024]{1,0:T(8,128)(2,1)} async-done(((bf16[1024,128]{1,0:T(8,128)(2,1)}), bf16[1024,1024]{1,0:T(8,128)(2,1)}) %all-gather.14.cloned.1.call-update) | async-done | bytes 2097168 | tf_op jit(solution)/shard_map/all_gather | solution.py:128
  169.8 17.6 %all_gather.37 = bf16[2,1024]{1,0:T(2,128)(2,1)S(1)} all-gather(bf16[2,128]{1,0:T(2,128)(2,1)S(1)} %copy-done.21), channel_id=1, replica_groups=mesh['dp'=8,'tensor'=4] {'dp'}, dimensions={1}, use_global_device_ids=true | all-gather | bytes 4608 | tf_op jit(solution)/shard_map/all_gather | solution.py:132
  187.4 38.5 %reduce-scatter.13.cloned.1.call-done = f32[3,1,128,1024]{3,2,0,1:T(8,128)} async-done(((f32[3,4,128,1024]{3,2,0,1:T(8,128)}), f32[3,1,128,1024]{3,2,0,1:T(8,128)}) %reduce-scatter.13.cloned.1.call-update) | async-done | bytes 1572880 | tf_op jit(solution)/shard_map/reduce_scatter | solution.py:170
  230.7 26.3 %all-gather = bf16[8,1,512]{2,1,0:T(2,128)(2,1)S(1)} all-gather(bf16[1,1,512]{2,1,0:T(2,128)(2,1)S(1)} %reshape.400), channel_id=1, replica_groups=mesh['dp'=8,'tensor'=4] {'dp'}, dimensions={0}, use_global_device_ids=true | all-gather | bytes 9216 | tf_op jit(solution)/shard_map/all_gather | solution.py:133
  261.9 47.7 %all-gather.18.cloned.1.call-done = bf16[1024,1024]{1,0:T(8,128)(2,1)} async-done(((bf16[128,1024]{1,0:T(8,128)(2,1)}), bf16[1024,1024]{1,0:T(8,128)(2,1)}) %all-gather.18.cloned.1.call-update) | async-done | bytes 2097168 | tf_op jit(solution)/shard_map/all_gather | solution.py:129
  309.5 8.4 multiply_convert_fusion.1
  317.9 43.5 %all-gather.20.cloned.1.call-done = bf16[1024,1024]{1,0:T(8,128)(2,1)} async-done(((bf16[1024,128]{1,0:T(8,128)(2,1)}), bf16[1024,1024]{1,0:T(8,128)(2,1)}) %all-gather.20.cloned.1.call-update) | async-done | bytes 2097168 | tf_op jit(solution)/shard_map/all_gather | solution.py:130
  373.8 19.7 %all-to-all-done.2 = bf16[24,1,16,1024]{3,2,1,0:T(8,128)(2,1)} async-done(((bf16[24,1,16,1024]{3,2,1,0:T(8,128)(2,1)}), bf16[24,1,16,1024]{3,2,1,0:T(8,128)(2,1)}, u32[]{:S(2)}, u32[]{:S(2)}) %all-to-all-start.2) | async-done | bytes 786464 | tf_op jit(solution)/shard_map/all_to_all | solution.py:120
  410.9 28.6 %all-gather.22.cloned.1.call-done = bf16[3,4,128,1024]{3,2,0,1:T(8,128)(2,1)} async-done(((bf16[3,1,128,1024]{3,2,0,1:T(8,128)(2,1)}), bf16[3,4,128,1024]{3,2,0,1:T(8,128)(2,1)}) %all-gather.22.cloned.1.call-update) | async-done | bytes 3145744 | tf_op jit(solution)/shard_map/all_gather | solution.py:203
  456.3 38.1 %reduce-scatter.17.cloned.1.call-done = bf16[3,1,128,1024]{3,2,0,1:T(8,128)(2,1)} async-done(((bf16[3,4,128,1024]{3,2,0,1:T(8,128)(2,1)}), bf16[3,1,128,1024]{3,2,0,1:T(8,128)(2,1)}) %reduce-scatter.17.cloned.1.call-update) | async-done | bytes 786448 | tf_op jit(solution)/shard_map/reduce_scatter | solution.py:216
  500.0 28.4 %all-gather.24.cloned.1.call-done = bf16[3,4,128,1024]{3,2,0,1:T(8,128)(2,1)} async-done(((bf16[3,1,128,1024]{3,2,0,1:T(8,128)(2,1)}), bf16[3,4,128,1024]{3,2,0,1:T(8,128)(2,1)}) %all-gather.24.cloned.1.call-update) | async-done | bytes 3145744 | tf_op jit(solution)/shard_map/all_gather | solution.py:223
  535.9 33.4 %while.27 = (s32[]{:T(128)}, bf16[3,512,256]{1,2,0:T(8,128)(2,1)}, bf16[3,512,256]{2,1,0:T(8,128)(2,1)}, bf16[3,512,256]{1,2,0:T(8,128)(2,1)}, bf16[3,512,256]{1...) while((s32[]{:T(128)}, bf16[3,512,256]{1,2,0:T(8,128)(2,1)}, ...), condition=%wide.region_18.19_spmd, body=%wide.region_16.18_spmd.sunk | while | flops 687471104 | bytes 38856864 | solution.py:230
  582.4 10.4 all-reduce.1
  634.8 22.0 %all-to-all-done.1 = bf16[3,1,128,1024]{3,0,1,2:T(4,128)(2,1)} async-done(((bf16[3,1,128,1024]{3,0,1,2:T(4,128)(2,1)}), bf16[3,1,128,1024]{3,0,1,2:T(4,128)(2,1)}, u32[]{:S(2)}, u32[]{:S(2)}) %all-to-all-start.1) | async-done | bytes 786464 | tf_op jit(solution)/shard_map/all_to_all | solution.py:281
  664.0 46.7 %all-reduce = f32[4096]{0:T(1024)S(1)} all-reduce(bf16[4096]{0:T(1024)(128)(2,1)S(1)} %get-tuple-element.254), channel_id=12, replica_groups=mesh['dp'=8,'tensor'=4] {'dp'}, use_global_device_ids=true, to_apply=%region_38.39.clone | all-reduce | flops 4096 | bytes 24576
  712.8 58.6 %reduce-scatter.21.cloned.1.call-done = f32[3,128,256]{1,2,0:T(8,128)} async-done(((f32[3,1024,256]{1,2,0:T(8,128)}), f32[3,128,256]{1,2,0:T(8,128)}) %reduce-scatter.21.cloned.1.call-update) | async-done | bytes 393232 | tf_op jit(solution)/shard_map/reduce_scatter | solution.py:272
  775.3 88.2 %reduce-scatter.27.cloned.1.call-done = f32[1024,128]{1,0:T(8,128)} async-done(((f32[1024,1024]{1,0:T(8,128)}), f32[1024,128]{1,0:T(8,128)}) %reduce-scatter.27.cloned.1.call-update) | async-done | bytes 524304 | tf_op jit(solution)/shard_map/reduce_scatter | solution.py:275
  863.5 91.9 %reduce-scatter.25.cloned.1.call-done = f32[128,1024]{1,0:T(8,128)} async-done(((f32[1024,1024]{1,0:T(8,128)}), f32[128,1024]{1,0:T(8,128)}) %reduce-scatter.25.cloned.1.call-update) | async-done | bytes 524304 | tf_op jit(solution)/shard_map/reduce_scatter | solution.py:274
  955.3 57.1 %reduce-scatter.29.cloned.1.call-done = f32[6,128]{1,0:T(8,128)} async-done(((f32[6,1024]{1,0:T(8,128)}), f32[6,128]{1,0:T(8,128)}) %reduce-scatter.29.cloned.1.call-update) | async-done | bytes 3088 | tf_op jit(solution)/shard_map/reduce_scatter | solution.py:276
  1012.5 67.2 %reduce-scatter.23.cloned.1.call-done = f32[256,128]{1,0:T(8,128)} async-done(((f32[256,1024]{1,0:T(8,128)}), f32[256,128]{1,0:T(8,128)}) %reduce-scatter.23.cloned.1.call-update) | async-done | bytes 131088 | tf_op jit(solution)/shard_map/reduce_scatter | solution.py:273
  (283 shorter events, 204.2 us)
Async XLA Ops:
  7.2 58.1 %all-gather.10.cloned.1.call-start = ((), (), s32[]{:S(2)}) async-start(), calls=%async_computation.14 | async-start | bytes 3932160 | tf_op jit(solution)/shard_map/all_gather | solution.py:154
  9.3 55.9 %copy-start.26 = (s32[24]{0:T(128)S(1)}, s32[24]{0:T(128)}, u32[]{:S(2)}) copy-start(s32[24]{0:T(128)} %param.17) | copy-start | bytes 292
  37.5 74.1 %all-gather.12.cloned.1.call-start = ((), (), s32[]{:S(2)}) async-start(), calls=%async_computation.15 | async-start | bytes 1769472 | tf_op jit(solution)/shard_map/all_gather | solution.py:127
  38.3 125.3 %all-gather.14.cloned.1.call-start = ((), (), s32[]{:S(2)}) async-start(), calls=%async_computation.16 | async-start | bytes 2359296 | tf_op jit(solution)/shard_map/all_gather | solution.py:128
  39.0 186.8 %reduce-scatter.13.cloned.1.call-start = ((), (), s32[]{:S(2)}) async-start(), calls=%async_computation.17 | async-start | bytes 7864320 | tf_op jit(solution)/shard_map/reduce_scatter | solution.py:170
  67.5 44.1 %copy-start.10 = (bf16[3,4,128,1024]{3,2,1,0:T(8,128)(2,1)}, bf16[3,4,128,1024]{3,2,1,0:T(8,128)(2,1)S(1)}, u32[]{:S(2)}) copy-start(bf16[3,4,128,1024]{3,2,1,0:T(8,128)(2,1)S(1)} %copy.102) | copy-start | bytes 9437188
  169.1 88.8 %all-gather.16.cloned.1.call-start = ((), (), s32[]{:S(2)}) async-start(), calls=%async_computation.18 | async-start | bytes 3932160 | tf_op jit(solution)/shard_map/all_gather | solution.py:175
  229.3 80.2 %all-gather.18.cloned.1.call-start = ((), (), s32[]{:S(2)}) async-start(), calls=%async_computation.19 | async-start | bytes 2359296 | tf_op jit(solution)/shard_map/all_gather | solution.py:129
  229.9 131.5 %all-gather.20.cloned.1.call-start = ((), (), s32[]{:S(2)}) async-start(), calls=%async_computation.20 | async-start | bytes 2359296 | tf_op jit(solution)/shard_map/all_gather | solution.py:130
  230.6 175.0 %reduce-scatter.15.cloned.1.call-start = ((), (), s32[]{:S(2)}) async-start(), calls=%async_computation.21 | async-start | bytes 3932160 | tf_op jit(solution)/shard_map/reduce_scatter | solution.py:188
  369.3 24.1 %all-to-all-start.2 = ((bf16[24,1,16,1024]{3,2,1,0:T(8,128)(2,1)}), bf16[24,1,16,1024]{3,2,1,0:T(8,128)(2,1)}, u32[]{:S(2)}, u32[]{:S(2)}) async-start(bf16[24,1,16,1024]{3,2,1,0:T(8,128)(2,1)} %param.16), calls=%async_computation.4 | async-start | bytes 1572864 | tf_op jit(solution)/shard_map/all_to_all | solution.py:120
  373.6 66.0 %all-gather.22.cloned.1.call-start = ((), (), s32[]{:S(2)}) async-start(), calls=%async_computation.22 | async-start | bytes 3932160 | tf_op jit(solution)/shard_map/all_gather | solution.py:203
  410.8 83.5 %reduce-scatter.17.cloned.1.call-start = ((), (), s32[]{:S(2)}) async-start(), calls=%async_computation.23 | async-start | bytes 3932160 | tf_op jit(solution)/shard_map/reduce_scatter | solution.py:216
  456.2 72.2 %all-gather.24.cloned.1.call-start = ((), (), s32[]{:S(2)}) async-start(), calls=%async_computation.24 | async-start | bytes 3932160 | tf_op jit(solution)/shard_map/all_gather | solution.py:223
  499.8 131.9 %reduce-scatter.19.cloned.1.call-start = ((), (), s32[]{:S(2)}) async-start(), calls=%async_computation.25 | async-start | bytes 3932160 | tf_op jit(solution)/shard_map/reduce_scatter | solution.py:246
  580.8 130.5 %reduce-scatter.31.cloned.1.call-start = ((), (), s32[]{:S(2)}) async-start(), calls=%async_computation.31 | async-start | bytes 589824
  593.8 177.6 %reduce-scatter.21.cloned.1.call-start = ((), (), s32[]{:S(2)}) async-start(), calls=%async_computation.26 | async-start | bytes 3538944 | tf_op jit(solution)/shard_map/reduce_scatter | solution.py:272
  600.7 262.8 %reduce-scatter.27.cloned.1.call-start = ((), (), s32[]{:S(2)}) async-start(), calls=%async_computation.29 | async-start | bytes 4718592 | tf_op jit(solution)/shard_map/reduce_scatter | solution.py:275
  609.5 345.8 %reduce-scatter.25.cloned.1.call-start = ((), (), s32[]{:S(2)}) async-start(), calls=%async_computation.28 | async-start | bytes 4718592 | tf_op jit(solution)/shard_map/reduce_scatter | solution.py:274
  621.2 35.6 %all-to-all-start.1 = ((bf16[3,1,128,1024]{3,0,1,2:T(4,128)(2,1)}), bf16[3,1,128,1024]{3,0,1,2:T(4,128)(2,1)}, u32[]{:S(2)}, u32[]{:S(2)}) async-start(bf16[3,1,128,1024]{3,0,1,2:T(4,128)(2,1)} %copy.110), calls=%async_computation.3 | async-start | bytes 2097152 | tf_op jit(solution)/shard_map/all_to_all | solution.py:281
  626.8 385.7 %reduce-scatter.29.cloned.1.call-start = ((), (), s32[]{:S(2)}) async-start(), calls=%async_computation.30 | async-start | bytes 36864 | tf_op jit(solution)/shard_map/reduce_scatter | solution.py:276
  627.5 452.2 %reduce-scatter.23.cloned.1.call-start = ((), (), s32[]{:S(2)}) async-start(), calls=%async_computation.27 | async-start | bytes 1179648 | tf_op jit(solution)/shard_map/reduce_scatter | solution.py:273
  656.8 116.6 %all-to-all-start.3 = ((bf16[3,1,128,1024]{3,0,1,2:T(4,128)(2,1)}), bf16[3,1,128,1024]{3,0,1,2:T(4,128)(2,1)S(1)}, u32[]{:S(2)}, u32[]{:S(2)}) async-start(bf16[3,1,128,1024]{3,0,1,2:T(4,128)(2,1)} %copy.124), calls=%async_computation.7 | async-start | bytes 2097152 | tf_op jit(solution)/shard_map/all_to_all | solution.py:282
  771.4 308.3 %copy-start.1 = (bf16[24,1,16,1024]{3,2,1,0:T(8,128)(2,1)S(1)}, bf16[24,1,16,1024]{3,2,1,0:T(8,128)(2,1)}, u32[]{:S(2)}) copy-start(bf16[24,1,16,1024]{3,2,1,0:T(8,128)(2,1)} %param.15) | copy-start | bytes 2359300
  (26 other events, 206.8 us)
Sparse Core Ops, SparseCore 0:
  37.6 27.5 all-gather.9
  67.4 44.1 all-gather.11
  113.7 49.8 all-gather.13
  169.3 56.5 reduce-scatter.12
  229.4 28.5 all-gather.15
  260.2 49.2 all-gather.17
  311.8 49.5 all-gather.19
  369.5 36.1 reduce-scatter.14
  411.0 28.5 all-gather.21
  456.3 37.9 reduce-scatter.16
  499.9 28.5 all-gather.23
  580.9 37.9 reduce-scatter.18
  622.3 71.7 reduce-scatter.30
  698.0 73.3 reduce-scatter.20
  775.9 87.5 reduce-scatter.26
  867.5 87.7 reduce-scatter.24
  959.2 53.2 reduce-scatter.28
  1016.7 62.9 reduce-scatter.22
where the time goes:
time: 1090 us
  waiting for transfers between devices  716 us (66%)
  blocking collectives  154 us (14%)
  matrix products  85.6 us (8%)
  local copies, waits for them, and re-layouts  71.8 us (7%)
  other arithmetic  28.6 us (3%)
  between operations  16 us (1%)
  starting transfers between devices  14.6 us (1%)
    reduce_scatter x1, waiting for transfers between devices, body(): lax.psum_scatter(expand_grad, 'dp', scatter_dimension=0, tiled=True)  91.9 us
    reduce_scatter x1, waiting for transfers between devices, body(): lax.psum_scatter(shrink_grad, 'dp', scatter_dimension=1, tiled=True)  88.2 us
    reduce_scatter x1, waiting for transfers between devices, body(): lax.psum_scatter(output_grad, 'dp', scatter_dimension=1, tiled=True)  67.2 us
    reduce_scatter x1, waiting for transfers between devices, body(): lax.psum_scatter(triple_grad, 'dp', scatter_dimension=1, tiled=True)  58.6 us
    reduce_scatter x1, waiting for transfers between devices, body(): lax.psum_scatter(bias_grad, 'dp', scatter_dimension=1, tiled=True)  57.1 us
    all_gather x1, waiting for transfers between devices, body(): lax.all_gather(expand_weight, 'dp', axis=0, tiled=True)  47.7 us
    unnamed x1, blocking collectives  46.7 us
    all_gather x1, waiting for transfers between devices, body(): lax.all_gather(triple_weight, 'dp', axis=1, tiled=True)  44.1 us
  transfers between devices with their start and end apart: 21, of which 17 were waited for; matrix products, arithmetic and copies ran while one was open for 7% of the time, Pallas kernels for 0%

commit v1 on v0

--- a/solution.py
+++ b/solution.py
@@ -1,8 +1,12 @@
+import functools
 import math
+import types
 
 import jax
 import jax.numpy as jnp
 from jax import lax
+from jax.experimental import pallas as pl
+from jax.experimental.pallas import tpu as pltpu
 from jax.sharding import PartitionSpec as P
 
 HEAD_DIM = 64
@@ -95,7 +99,7 @@
     )
 
 
-def body(
+def plain_body(
     tokens,
     cotangent,
     lengths,
@@ -293,6 +297,967 @@
         shards[4],
         shards[5],
         shards[6],
+    )
+
+
+BF = jnp.bfloat16
+F32 = jnp.float32
+MESH = pl.DeviceIdType.MESH
+LOG2E = math.log2(math.e)
+N_SEM = 320
+VMEM_BYTES = 64 * 1024 * 1024
+
+
+def mm(a, b):
+    return lax.dot_general(a, b, (((1,), (0,)), ((), ())), preferred_element_type=F32)
+
+
+def mm_t(a, b):
+    return lax.dot_general(a, b, (((1,), (1,)), ((), ())), preferred_element_type=F32)
+
+
+def t_mm(a, b):
+    return lax.dot_general(a, b, (((0,), (0,)), ((), ())), preferred_element_type=F32)
+
+
+class Links:
+    def __init__(self, send_sems, recv_sems, local_sems):
+        self.send_sems = send_sems
+        self.recv_sems = recv_sems
+        self.local_sems = local_sems
+        self.slots = {}
+        self.flying = {}
+        self.local_count = 0
+
+    def slot(self, name):
+        return self.slots.setdefault(name, len(self.slots))
+
+    def send(self, name, src, dst, where):
+        i = self.slot(name)
+        copy = pltpu.make_async_remote_copy(
+            src_ref=src,
+            dst_ref=dst,
+            send_sem=self.send_sems.at[i],
+            recv_sem=self.recv_sems.at[i],
+            device_id=where,
+            device_id_type=MESH,
+        )
+        copy.start()
+        self.flying[name] = copy
+
+    def sent(self, name):
+        self.flying.pop(name).wait_send()
+
+    def arrived(self, name, dst, where):
+        i = self.slot(name)
+        pltpu.make_async_remote_copy(
+            src_ref=dst,
+            dst_ref=dst,
+            send_sem=self.send_sems.at[i],
+            recv_sem=self.recv_sems.at[i],
+            device_id=where,
+            device_id_type=MESH,
+        ).wait_recv()
+
+    def local(self, src, dst):
+        copy = pltpu.make_async_copy(src, dst, self.local_sems.at[self.local_count])
+        self.local_count += 1
+        copy.start()
+        return copy
+
+
+def layer_kernel(g, *refs):
+    (order_s, inverse_s, lengths_s, tok, cot, w3, wo, we, ws, pack) = refs[:10]
+    (out_mixed, out_back, out_g3, out_go, out_ge, out_gs, out_small) = refs[10:17]
+    s = types.SimpleNamespace(**dict(zip(g.scratch_names, refs[17:])))
+    n_seq, quarter, width = g.n_seq, g.quarter, g.width
+    n_dp, n_y, n_t = g.n_dp, g.n_y, g.n_t
+    n_z = n_dp // n_y
+    full = n_t * quarter
+    half = full // 2
+    rows = quarter // n_dp
+    hw, fw = g.head_width, g.hidden_width
+    heads = hw // HEAD_DIM
+    dw = width // n_dp
+    tile = 256
+    ebias_rows = g.ebias_rows
+    owners = n_dp // n_t
+
+    d = lax.axis_index("dp")
+    t = lax.axis_index("tensor")
+    z, y = d // n_y, d % n_y
+    x, c = t // 2, t % 2
+    t_core = x * 2 + (1 - c)
+    t_far = (1 - x) * 2 + c
+    t_diag = (1 - x) * 2 + (1 - c)
+
+    def dp_to(o):
+        return (d + o) % n_dp
+
+    def dp_from(o):
+        return (d + n_dp - o) % n_dp
+
+    def z_to(k):
+        return ((z + k) % n_z) * n_y + y
+
+    def z_from(k):
+        return ((z + n_z - k) % n_z) * n_y + y
+
+    y_peer = z * n_y + (1 - y)
+    link = Links(s.send_sems, s.recv_sems, s.local_sems)
+
+    barrier = pltpu.get_barrier_semaphore()
+    for o in range(1, n_dp):
+        pl.semaphore_signal(barrier, inc=1, device_id={"dp": dp_to(o)}, device_id_type=MESH)
+    for peer in (t_core, t_far, t_diag):
+        pl.semaphore_signal(barrier, inc=1, device_id={"tensor": peer}, device_id_type=MESH)
+
+    stage, x_all, cots = s.stage, s.x_all, s.cots
+    w3_all, wo_all, we_all, ws_all = s.w3_all, s.wo_all, s.we_all, s.ws_all
+    pack_all, vec, ebias = s.pack_all, s.vec, s.ebias
+    qkv, att, lse, part = s.qkv, s.att, s.lse, s.part
+    r_a, r_b, r_x = s.r_a, s.r_b, s.r_x
+    n1, inv1, u_all, hid, slope = s.n1, s.inv1, s.u_all, s.hid, s.slope
+    dz, dh, dy, dqkv = s.dz, s.dh, s.dy, s.dqkv
+    acc, hacc, qacc = s.acc, s.hacc, s.qacc
+    kt, ot, dk_acc, dv_acc, da = s.kt, s.ot, s.dk_acc, s.dv_acc, s.da
+    mixed_send, back_send, back_recv = s.mixed_send, s.back_send, s.back_recv
+
+    def al(v, m):
+        return pl.multiple_of(v, m)
+
+    def seq_rows(j, start, n):
+        return pl.ds(al(j * full + start, 16), n)
+
+    def mine(j):
+        return seq_rows(j, t * quarter, quarter)
+
+
+    def permute(k, carry):
+        stage[k] = tok[inverse_s[k]]
+        return carry
+
+    lax.fori_loop(0, n_dp * n_seq, permute, 0)
+    acc[...] = jnp.zeros_like(acc)
+    hacc[...] = jnp.zeros_like(hacc)
+    qacc[...] = jnp.zeros_like(qacc)
+    pl.semaphore_wait(barrier, n_dp - 1 + 3)
+
+    def x_block(j, src):
+        return x_all.at[seq_rows(j, t * quarter + src * rows, rows)]
+
+    def tokens_start(j):
+        for o in range(1, n_dp):
+            e = dp_to(o)
+            link.send(("tok", j, o), stage.at[e * n_seq + j], x_block(j, d), {"dp": e})
+        x_all[seq_rows(j, t * quarter + d * rows, rows), :] = stage[d * n_seq + j]
+
+    def tokens_finish(j):
+        for o in range(1, n_dp):
+            link.arrived(("tok", j, o), x_block(j, dp_from(o)), {"dp": dp_from(o)})
+            link.sent(("tok", j, o))
+
+    def cot_block(src):
+        return cots.at[:, pl.ds(al(src * rows, 16), rows), :]
+
+    def cot_start():
+        for o in range(1, n_dp):
+            e = dp_to(o)
+            link.send(("cot", o), cot.at[pl.ds(e * n_seq, n_seq)], cot_block(d), {"dp": e})
+        own = link.local(cot.at[pl.ds(d * n_seq, n_seq)], cot_block(d))
+        return own
+
+    def cot_finish(own):
+        own.wait()
+        for o in range(1, n_dp):
+            link.arrived(("cot", o), cot_block(dp_from(o)), {"dp": dp_from(o)})
+            link.sent(("cot", o))
+
+    def cols(ref, e):
+        return ref.at[:, pl.ds(al(e * dw, 128), dw)]
+
+    def row_block(ref, e):
+        return ref.at[pl.ds(al(e * dw, 16), dw), :]
+
+    gathers = {
+        "pack": (pack, lambda e: cols(pack_all, e)),
+        "w3": (w3, lambda e: row_block(w3_all, e)),
+        "wo": (wo.at[pl.ds(al(t * hw, 16), hw), :], lambda e: cols(wo_all, e)),
+        "we": (we, lambda e: row_block(we_all, e)),
+        "ws": (ws, lambda e: cols(ws_all, e)),
+    }
+    own_copies = {}
+
+    def gather_start(name):
+        src, block = gathers[name]
+        for k in range(1, n_z):
+            link.send((name, "z", k), src, block(d), {"dp": z_to(k)})
+        link.send((name, "y", 0), src, block(d), {"dp": y_peer})
+        own_copies[name] = link.local(src, block(d))
+
+    def gather_forward(name, k):
+        _, block = gathers[name]
+        e = z_from(k)
+        link.arrived((name, "z", k), block(e), {"dp": e})
+        link.send((name, "y", k), block(e), block(e), {"dp": y_peer})
+
+    def gather_finish(name):
+        _, block = gathers[name]
+        own_copies.pop(name).wait()
+        for k in range(n_z):
+            e = ((z + n_z - k) % n_z) * n_y + (1 - y)
+            link.arrived((name, "y", k), block(e), {"dp": y_peer})
+        for k in range(1, n_z):
+            link.sent((name, "z", k))
+        for k in range(n_z):
+            link.sent((name, "y", k))
+
+
+    def t_rows(j, who):
+        return seq_rows(j, who * quarter, quarter)
+
+    def ag_start(buf, tag, j):
+        own = buf.at[t_rows(j, t)]
+        link.send((tag, "far", j), own, own, {"tensor": t_far})
+        link.send((tag, "core", j), own, own, {"tensor": t_core})
+
+    def ag_forward(buf, tag, j):
+        got = buf.at[t_rows(j, t_far)]
+        link.arrived((tag, "far", j), got, {"tensor": t_far})
+        link.send((tag, "fwd", j), got, got, {"tensor": t_core})
+
+    def ag_finish(buf, tag, j):
+        link.arrived((tag, "core", j), buf.at[t_rows(j, t_core)], {"tensor": t_core})
+        link.arrived((tag, "fwd", j), buf.at[t_rows(j, t_diag)], {"tensor": t_core})
+        for what in ("far", "core", "fwd"):
+            link.sent((tag, what, j))
+
+    def q_rows(j):
+        return pl.ds(j * quarter, quarter)
+
+    def rs_start_far(tag, j):
+        link.send((tag, "b", j), part.at[t_rows(j, t_diag)], r_b.at[q_rows(j)], {"tensor": t_core})
+
+    def rs_start_near(tag, j):
+        link.send((tag, "a", j), part.at[t_rows(j, t_core)], r_a.at[q_rows(j)], {"tensor": t_core})
+
+    def rs_forward(tag, j):
+        link.arrived((tag, "b", j), r_b.at[q_rows(j)], {"tensor": t_core})
+        far = t_rows(j, t_far)
+        both = part[far, :].astype(F32) + r_b[q_rows(j), :].astype(F32)
+        part[far, :] = both.astype(BF)
+        link.send((tag, "x", j), part.at[far], r_x.at[q_rows(j)], {"tensor": t_far})
+
+    def rs_finish(tag, j):
+        link.arrived((tag, "a", j), r_a.at[q_rows(j)], {"tensor": t_core})
+        link.arrived((tag, "x", j), r_x.at[q_rows(j)], {"tensor": t_far})
+        for what in ("a", "b", "x"):
+            link.sent((tag, what, j))
+
+    chunk = 32
+
+    def row_loop(fn):
+        lax.fori_loop(0, quarter // chunk, lambda i, carry: fn(i * chunk) or carry, 0)
+
+    def summed(j, r):
+        loc = seq_rows(j, t * quarter + r, chunk)
+        buf = pl.ds(al(j * quarter + r, 16), chunk)
+        return (
+            part[loc, :].astype(F32)
+            + r_a[buf, :].astype(F32)
+            + r_x[buf, :].astype(F32)
+        )
+
+    def add_sum(row, value):
+        acc[row : row + 1, :] += jnp.sum(value, axis=0, keepdims=True)
+
+    def two_halves(tag, j, fn):
+        fn(al(j * full + (1 - x) * half, 16))
+        rs_start_far(tag, j)
+        fn(al(j * full + x * half, 16))
+        rs_start_near(tag, j)
+
+    def by_tiles(n, fn):
+        lax.fori_loop(0, n // tile, lambda i, carry: fn(al(i * tile, tile)) or carry, 0)
+
+
+    def spread_vectors():
+        vec[...] = pack_all[...].astype(F32)
+        for i in range(owners):
+            e = t * owners + i
+            for r in range(ebias_rows):
+                ebias[0:1, (i * ebias_rows + r) * dw : (i * ebias_rows + r + 1) * dw] = vec[
+                    8 + r : 9 + r, pl.ds(al(e * dw, 128), dw)
+                ]
+
+
+    def project(j):
+        at = pl.ds(j * full, full)
+        for w in range(3):
+            span = slice(w * hw, (w + 1) * hw)
+            value = mm(x_all[at, :], w3_all[:, span])
+            if w == 0:
+                value = value + vec[0:1, pl.ds(al(t * hw, 128), hw)]
+            if w == 2:
+                value = value + vec[1:2, pl.ds(al(t * hw, 128), hw)]
+            qkv[at, span] = value.astype(BF)
+
+    lane_head = lax.broadcasted_iota(jnp.int32, (full, hw), 1) // HEAD_DIM
+    scale2 = LOG2E / math.sqrt(HEAD_DIM)
+
+    def head_scores(j, h, at):
+        q_head = jnp.where(lane_head == h, qkv[at, 0:hw], jnp.zeros((), BF))
+        raw = mm_t(qkv[at, hw : 2 * hw], q_head)
+        key_row = lax.broadcasted_iota(jnp.int32, (full, 1), 0)
+        visible = key_row < lengths_s[d * n_seq + j]
+        return q_head, jnp.where(visible, raw * scale2, MASKED)
+
+    def attention(j):
+        at = pl.ds(j * full, full)
+        kt[...] = jnp.transpose(qkv[at, 2 * hw : 3 * hw])
+
+        def head(h, carry):
+            span = pl.ds(al(h * HEAD_DIM, HEAD_DIM), HEAD_DIM)
+            _, scores = head_scores(j, h, at)
+            top = jnp.max(scores, axis=0, keepdims=True)
+            e = jnp.exp2(scores - top)
+            total = jnp.sum(e, axis=0, keepdims=True)
+            o = mm(kt[span, :], e.astype(BF))
+            ot[span, :] = o * (1.0 / total)
+            lse[j, pl.ds(h, 1), :] = top + jnp.log2(total)
+            return carry
+
+        lax.fori_loop(0, heads, head, 0)
+        att[at, :] = jnp.transpose(ot[...]).astype(BF)
+
+    def project_out(j):
+        def part_rows(start):
+            def go(n):
+                part[pl.ds(start, half), pl.ds(n, tile)] = mm(
+                    att[pl.ds(start, half), :], wo_all[:, pl.ds(n, tile)]
+                ).astype(BF)
+
+            by_tiles(width, go)
+
+        two_halves("r1", j, part_rows)
+
+    def norm_first(j):
+        def go(r):
+            loc = seq_rows(j, t * quarter + r, chunk)
+            buf = pl.ds(al(j * quarter + r, 16), chunk)
+            h = x_all[loc, :].astype(F32) + (summed(j, r) + vec[2:3, :])
+            center = h - jnp.mean(h, axis=-1, keepdims=True)
+            inv = lax.rsqrt(jnp.mean(center * center, axis=-1, keepdims=True) + EPSILON)
+            scaled = center * inv
+            n1[buf, :] = scaled
+            inv1[buf, :] = jnp.broadcast_to(inv, (chunk, 128))
+            u_all[loc, :] = (scaled * vec[6:7, :] + vec[3:4, :]).astype(BF)
+
+        row_loop(go)
+
+    def widen(j):
+        at = pl.ds(j * full, full)
+
+        def go(n):
+            f = mm(u_all[at, :], we_all[:, pl.ds(n, tile)]) + ebias[0:1, pl.ds(n, tile)]
+            cdf = 0.5 + 0.5 * lax.erf(f * (1.0 / math.sqrt(2.0)))
+            hid[at, pl.ds(n, tile)] = (f * cdf).astype(BF)
+            bell = jnp.exp2((f * f) * (-0.5 * LOG2E)) * (1.0 / math.sqrt(2.0 * math.pi))
+            slope[at, pl.ds(n, tile)] = (cdf + f * bell).astype(BF)
+
+        by_tiles(fw, go)
+
+    def shrink_rows(j):
+        def part_rows(start):
+            def go(n):
+                part[pl.ds(start, half), pl.ds(n, tile)] = mm(
+                    hid[pl.ds(start, half), :], ws_all[:, pl.ds(n, tile)]
+                ).astype(BF)
+
+            by_tiles(width, go)
+
+        two_halves("r2", j, part_rows)
+
+    def norm_second(j):
+        length = lengths_s[d * n_seq + j]
+
+        def go(r):
+            loc = seq_rows(j, t * quarter + r, chunk)
+            buf = pl.ds(al(j * quarter + r, 16), chunk)
+            u = n1[buf, :] * vec[6:7, :] + vec[3:4, :]
+            total = u + (summed(j, r) + vec[4:5, :])
+            center = total - jnp.mean(total, axis=-1, keepdims=True)
+            inv = lax.rsqrt(jnp.mean(center * center, axis=-1, keepdims=True) + EPSILON)
+            scaled = center * inv
+            mixed_send[buf, :] = (scaled * vec[7:8, :] + vec[5:6, :]).astype(BF)
+            place = t * quarter + r + lax.broadcasted_iota(jnp.int32, (chunk, 1), 0)
+            valid = (place < length).astype(F32)
+            e = cots[j, pl.ds(al(r, 16), chunk), :].astype(F32) * valid
+            add_sum(5, e)
+            add_sum(7, e * scaled)
+            pushed = e * vec[7:8, :]
+            first = jnp.mean(pushed, axis=-1, keepdims=True)
+            second = jnp.mean(pushed * scaled, axis=-1, keepdims=True)
+            grad = inv * (pushed - first - scaled * second)
+            add_sum(4, grad)
+            dy[buf, :] = grad
+            dz[loc, :] = grad.astype(BF)
+
+        row_loop(go)
+
+    def rows_out(tag, j, src, dst):
+        for o in range(1, n_dp):
+            e = dp_to(o)
+            link.send(
+                (tag, j, o),
+                src.at[pl.ds(al(j * quarter + e * rows, 16), rows)],
+                dst.at[d * n_seq + j],
+                {"dp": e},
+            )
+        return link.local(
+            src.at[pl.ds(al(j * quarter + d * rows, 16), rows)], dst.at[d * n_seq + j]
+        )
+
+    def rows_in(tag, j, dst, own):
+        own.wait()
+        for o in range(1, n_dp):
+            e = dp_from(o)
+            link.arrived((tag, j, o), dst.at[e * n_seq + j], {"dp": e})
+            link.sent((tag, j, o))
+
+
+    def widen_back(j):
+        at = pl.ds(j * full, full)
+
+        def go(n):
+            spread = mm_t(dz[at, :], ws_all[pl.ds(n, tile), :])
+            grad = (spread * slope[at, pl.ds(n, tile)].astype(F32)).astype(BF)
+            slope[at, pl.ds(n, tile)] = grad
+            hacc[0:1, pl.ds(n, tile)] += jnp.sum(grad.astype(F32), axis=0, keepdims=True)
+
+        by_tiles(fw, go)
+
+    def normed_rows(j):
+        def part_rows(start):
+            def go(n):
+                part[pl.ds(start, half), pl.ds(n, tile)] = mm_t(
+                    slope[pl.ds(start, half), :], we_all[pl.ds(n, tile), :]
+                ).astype(BF)
+
+            by_tiles(width, go)
+
+        two_halves("r3", j, part_rows)
+
+    def norm_first_back(j):
+        def go(r):
+            loc = seq_rows(j, t * quarter + r, chunk)
+            buf = pl.ds(al(j * quarter + r, 16), chunk)
+            du = dy[buf, :] + summed(j, r)
+            scaled = n1[buf, :]
+            add_sum(3, du)
+            add_sum(6, du * scaled)
+            pushed = du * vec[6:7, :]
+            first = jnp.mean(pushed, axis=-1, keepdims=True)
+            second = jnp.mean(pushed * scaled, axis=-1, keepdims=True)
+            grad = inv1[buf, 0:1] * (pushed - first - scaled * second)
+            add_sum(2, grad)
+            dy[buf, :] = grad
+            dh[loc, :] = grad.astype(BF)
+
+        row_loop(go)
+
+    def attention_back(j, between=None):
+        at = pl.ds(j * full, full)
+        da[...] = mm_t(dh[at, :], wo_all[...]).astype(BF)
+        kt[...] = jnp.transpose(qkv[at, hw : 2 * hw])
+        dk_acc[...] = jnp.zeros_like(dk_acc)
+        dv_acc[...] = jnp.zeros_like(dv_acc)
+
+        def head(h, carry):
+            span = pl.ds(al(h * HEAD_DIM, HEAD_DIM), HEAD_DIM)
+            q_head, scores = head_scores(j, h, at)
+            da_head = jnp.where(lane_head == h, da[...], jnp.zeros((), BF))
+            p = jnp.exp2(scores - lse[j, pl.ds(h, 1), :])
+            dp = mm_t(qkv[at, 2 * hw : 3 * hw], da_head)
+            inner = jnp.sum(p * dp, axis=0, keepdims=True)
+            ds = (p * (dp - inner)).astype(BF)
+            dv_acc[...] += mm(p.astype(BF), da_head)
+            dk_acc[...] += mm(ds, q_head)
+            ot[span, :] = mm(kt[span, :], ds)
+            return carry
+
+        lax.fori_loop(0, heads, head, 0)
+        scale = 1.0 / math.sqrt(HEAD_DIM)
+        grad_q = (jnp.transpose(ot[...]) * scale).astype(BF)
+        grad_k = (dk_acc[...] * scale).astype(BF)
+        grad_v = dv_acc[...].astype(BF)
+        dqkv[at, 0:hw] = grad_q
+        dqkv[at, hw : 2 * hw] = grad_k
+        dqkv[at, 2 * hw : 3 * hw] = grad_v
+        qacc[0:1, :] += jnp.sum(grad_q.astype(F32), axis=0, keepdims=True)
+        qacc[1:2, :] += jnp.sum(grad_v.astype(F32), axis=0, keepdims=True)
+
+    def token_rows(j):
+        def part_rows(start):
+            def go(n):
+                part[pl.ds(start, half), pl.ds(n, tile)] = mm_t(
+                    dqkv[pl.ds(start, half), :], w3_all[pl.ds(n, tile), :]
+                ).astype(BF)
+
+            by_tiles(width, go)
+
+        two_halves("r4", j, part_rows)
+
+    def finish_rows(j):
+        def go(r):
+            buf = pl.ds(al(j * quarter + r, 16), chunk)
+            back_send[buf, :] = (dy[buf, :] + summed(j, r)).astype(BF)
+
+        row_loop(go)
+
+
+    def weight_grad(dst, left, right):
+        n = dst.shape[0]
+
+        def go(m):
+            dst[pl.ds(m, tile), :] = t_mm(left[:, pl.ds(m, tile)], right[...]).astype(BF)
+
+        by_tiles(n, go)
+
+    grads = {
+        "gs": (s.gs, s.gs_y, s.gs_z, False, out_gs),
+        "ge": (s.ge, s.ge_y, s.ge_z, True, out_ge),
+        "go": (s.go, s.go_y, s.go_z, False, out_go),
+        "g3": (s.g3, s.g3_y, s.g3_z, True, out_g3),
+    }
+
+    def part_of(ref, by_rows, i):
+        if by_rows:
+            return (pl.ds(al(i * dw, 16), dw), slice(None))
+        return (slice(None), pl.ds(al(i * dw, 128), dw))
+
+    def grad_start(name):
+        whole, from_y, _, by_rows, _ = grads[name]
+        for k in list(range(1, n_z)) + [0]:
+            owner = ((z + k) % n_z) * n_y + (1 - y)
+            link.send(
+                (name, "y", k),
+                whole.at[part_of(whole, by_rows, owner)],
+                from_y.at[part_of(from_y, by_rows, k)],
+                {"dp": y_peer},
+            )
+
+    def grad_forward(name):
+        whole, from_y, from_z, by_rows, _ = grads[name]
+        for k in list(range(1, n_z)) + [0]:
+            mid = part_of(from_y, by_rows, k)
+            link.arrived((name, "y", k), from_y.at[mid], {"dp": y_peer})
+            owner = ((z + k) % n_z) * n_y + y
+            both = whole[part_of(whole, by_rows, owner)].astype(F32) + from_y[mid].astype(F32)
+            from_y[mid] = both.astype(BF)
+            if k:
+                link.send(
+                    (name, "z", k),
+                    from_y.at[mid],
+                    from_z.at[part_of(from_z, by_rows, k - 1)],
+                    {"dp": z_to(k)},
+                )
+
+    def grad_finish(name):
+        _, from_y, from_z, by_rows, out = grads[name]
+        total = from_y[part_of(from_y, by_rows, 0)].astype(F32)
+        for k in range(1, n_z):
+            at = part_of(from_z, by_rows, k - 1)
+            link.arrived((name, "z", k), from_z.at[at], {"dp": z_from(k)})
+            total = total + from_z[at].astype(F32)
+        out[...] = total
+        for k in range(1, n_z):
+            link.sent((name, "z", k))
+        for k in range(n_z):
+            link.sent((name, "y", k))
+
+    small_send, small_recv, small_t = s.small_send, s.small_recv, s.small_t
+
+    def small_start():
+        small_send[...] = jnp.zeros_like(small_send)
+        for e in range(n_dp):
+            small_send[e, 2:8, :] = acc[2:8, e * dw : (e + 1) * dw]
+        for i in range(owners):
+            e = t * owners + i
+            small_send[e, 0:2, :] = qacc[0:2, i * dw : (i + 1) * dw]
+            for r in range(ebias_rows):
+                at = (i * ebias_rows + r) * dw
+                small_send[e, 8 + r : 9 + r, :] = hacc[0:1, at : at + dw]
+        for o in range(1, n_dp):
+            e = dp_to(o)
+            link.send(("small", o), small_send.at[e], small_recv.at[o], {"dp": e})
+
+    def small_forward():
+        total = small_send[d]
+        for o in range(1, n_dp):
+            link.arrived(("small", o), small_recv.at[o], {"dp": dp_from(o)})
+            total = total + small_recv[o]
+            link.sent(("small", o))
+        small_t[t] = total
+        for what, peer in (("c", t_core), ("f", t_far), ("g", t_diag)):
+            link.send(("small_t", what), small_t.at[t], small_t.at[t], {"tensor": peer})
+
+    def small_finish():
+        for what, peer in (("c", t_core), ("f", t_far), ("g", t_diag)):
+            link.arrived(("small_t", what), small_t.at[peer], {"tensor": peer})
+            link.sent(("small_t", what))
+        total = small_t[0]
+        for i in range(1, n_t):
+            total = total + small_t[i]
+        out_small[...] = total
+
+
+    def reduce_pair(tag, j):
+        rs_finish(tag, j)
+
+    seqs = range(n_seq)
+    last = n_seq - 1
+    tokens_start(0)
+    gather_start("pack")
+    gather_start("w3")
+    for j in seqs[1:]:
+        tokens_start(j)
+    gather_start("wo")
+    tokens_finish(0)
+    ag_start(x_all, "x", 0)
+    for k in range(1, n_z):
+        gather_forward("pack", k)
+        gather_forward("w3", k)
+    for j in seqs[1:]:
+        tokens_finish(j)
+        ag_start(x_all, "x", j)
+    for k in range(1, n_z):
+        gather_forward("wo", k)
+    for j in seqs:
+        ag_forward(x_all, "x", j)
+    gather_finish("pack")
+    spread_vectors()
+    gather_finish("w3")
+    gather_start("we")
+    gather_start("ws")
+    ag_finish(x_all, "x", 0)
+    project(0)
+    attention(0)
+    for k in range(1, n_z):
+        gather_forward("we", k)
+    gather_finish("wo")
+    project_out(0)
+    ag_finish(x_all, "x", 1)
+    project(1)
+    rs_forward("r1", 0)
+    attention(1)
+    for k in range(1, n_z):
+        gather_forward("ws", k)
+    cot_own = cot_start()
+    project_out(1)
+    rs_finish("r1", 0)
+    norm_first(0)
+    ag_start(u_all, "u", 0)
+    ag_finish(x_all, "x", 2)
+    project(2)
+    rs_forward("r1", 1)
+    attention(2)
+    ag_forward(u_all, "u", 0)
+    project_out(2)
+    rs_finish("r1", 1)
+    norm_first(1)
+    ag_start(u_all, "u", 1)
+    gather_finish("we")
+    ag_finish(u_all, "u", 0)
+    rs_forward("r1", 2)
+    widen(0)
+    ag_forward(u_all, "u", 1)
+    gather_finish("ws")
+    shrink_rows(0)
+    rs_finish("r1", 2)
+    norm_first(2)
+    ag_start(u_all, "u", 2)
+    ag_finish(u_all, "u", 1)
+    rs_forward("r2", 0)
+    widen(1)
+    ag_forward(u_all, "u", 2)
+    cot_finish(cot_own)
+    shrink_rows(1)
+    mixed_own = []
+    rs_finish("r2", 0)
+    norm_second(0)
+    ag_start(dz, "z", 0)
+    ag_finish(u_all, "u", 2)
+    rs_forward("r2", 1)
+    widen(2)
+    ag_forward(dz, "z", 0)
+    shrink_rows(2)
+    rs_finish("r2", 1)
+    norm_second(1)
+    ag_start(dz, "z", 1)
+    ag_finish(dz, "z", 0)
+    rs_forward("r2", 2)
+    widen_back(0)
+    ag_forward(dz, "z", 1)
+    normed_rows(0)
+    rs_finish("r2", 2)
+    norm_second(2)
+    ag_start(dz, "z", 2)
+    for j in seqs:
+        mixed_own.append(rows_out("mix", j, mixed_send, out_mixed))
+    ag_finish(dz, "z", 1)
+    rs_forward("r3", 0)
+    widen_back(1)
+    ag_forward(dz, "z", 2)
+    normed_rows(1)
+    rs_finish("r3", 0)
+    norm_first_back(0)
+    ag_start(dh, "h", 0)
+    ag_finish(dz, "z", 2)
+    rs_forward("r3", 1)
+    widen_back(2)
+    ag_forward(dh, "h", 0)
+    normed_rows(2)
+    rs_finish("r3", 1)
+    norm_first_back(1)
+    ag_start(dh, "h", 1)
+    weight_grad(s.gs, hid, dz)
+    grad_start("gs")
+    rs_forward("r3", 2)
+    ag_forward(dh, "h", 1)
+    ag_finish(dh, "h", 0)
+    attention_back(0)
+    rs_finish("r3", 2)
+    norm_first_back(2)
+    ag_start(dh, "h", 2)
+    token_rows(0)
+    grad_forward("gs")
+    weight_grad(s.ge, u_all, slope)
+    grad_start("ge")
+    rs_forward("r4", 0)
+    ag_forward(dh, "h", 2)
+    ag_finish(dh, "h", 1)
+    attention_back(1)
+    rs_finish("r4", 0)
+    finish_rows(0)
+    back_own = [rows_out("back", 0, back_send, back_recv)]
+    token_rows(1)
+    grad_forward("ge")
+    ag_finish(dh, "h", 2)
+    rs_forward("r4", 1)
+    attention_back(2)
+    weight_grad(s.g3, x_all, dqkv)
+    grad_start("g3")
+    token_rows(2)
+    rs_finish("r4", 1)
+    finish_rows(1)
+    back_own.append(rows_out("back", 1, back_send, back_recv))
+    rs_forward("r4", 2)
+    grad_forward("g3")
+    small_start()
+    weight_grad(s.go, att, dh)
+    grad_start("go")
+    rs_finish("r4", 2)
+    finish_rows(2)
+    back_own.append(rows_out("back", 2, back_send, back_recv))
+    grad_finish("gs")
+    grad_finish("ge")
+    for j in seqs:
+        rows_in("mix", j, out_mixed, mixed_own[j])
+    small_forward()
+    grad_forward("go")
+    grad_finish("g3")
+    small_finish()
+    grad_finish("go")
+    for j in seqs:
+        rows_in("back", j, back_recv, back_own[j])
+
+    def restore(k, carry):
+        out_back[k] = back_recv[order_s[k]]
+        return carry
+
+    lax.fori_loop(0, n_dp * n_seq, restore, 0)
+
+
+def body(
+    tokens,
+    cotangent,
+    lengths,
+    order,
+    triple_weight,
+    output_weight,
+    expand_weight,
+    shrink_weight,
+    biases,
+    gains,
+    expand_bias,
+):
+    n_dp, n_t = lax.axis_size("dp"), lax.axis_size("tensor")
+    slots, _, rows, width = tokens.shape
+    n_seq = slots // n_dp
+    quarter = rows * n_dp
+    full = quarter * n_t
+    dw = triple_weight.shape[1]
+    hw = triple_weight.shape[2]
+    fw = expand_weight.shape[1]
+    fits = (
+        n_t == 4
+        and n_dp % 4 == 0
+        and rows % 16 == 0
+        and dw % 128 == 0
+        and hw % 128 == 0
+        and n_seq == 3
+        and expand_bias.shape[0] % dw == 0
+        and n_dp % n_t == 0
+    )
+    if not fits:
+        return plain_body(
+            tokens,
+            cotangent,
+            lengths,
+            order,
+            triple_weight,
+            output_weight,
+            expand_weight,
+            shrink_weight,
+            biases,
+            gains,
+            expand_bias,
+        )
+    n_y = 2
+    n_z = n_dp // n_y
+    ebias_rows = expand_bias.shape[0] // dw
+    ids = jnp.arange(slots, dtype=jnp.int32)
+    inverse = jnp.sum(jnp.where(order[None, :] == ids[:, None], ids[None, :], 0), axis=1)
+    pack_rows = 16
+    pack = jnp.concatenate(
+        [
+            biases,
+            gains,
+            expand_bias.reshape(ebias_rows, dw),
+            jnp.zeros((pack_rows - 8 - ebias_rows, dw), BF),
+        ]
+    )
+    w3 = jnp.concatenate([triple_weight[0], triple_weight[1], triple_weight[2]], axis=1)
+    all_rows = n_seq * full
+    own_rows = n_seq * quarter
+    vm = pltpu.VMEM
+    scratch = dict(
+        stage=vm((slots, rows, width), BF),
+        x_all=vm((all_rows, width), BF),
+        cots=vm((n_seq, quarter, width), BF),
+        w3_all=vm((width, 3 * hw), BF),
+        wo_all=vm((hw, width), BF),
+        we_all=vm((width, fw), BF),
+        ws_all=vm((fw, width), BF),
+        pack_all=vm((pack_rows, width), BF),
+        vec=vm((pack_rows, width), F32),
+        ebias=vm((8, fw), F32),
+        qkv=vm((all_rows, 3 * hw), BF),
+        att=vm((all_rows, hw), BF),
+        lse=vm((n_seq, 8, full), F32),
+        part=vm((all_rows, width), BF),
+        r_a=vm((own_rows, width), BF),
+        r_b=vm((own_rows, width), BF),
+        r_x=vm((own_rows, width), BF),
+        n1=vm((own_rows, width), F32),
+        inv1=vm((own_rows, 128), F32),
+        u_all=vm((all_rows, width), BF),
+        hid=vm((all_rows, fw), BF),
+        slope=vm((all_rows, fw), BF),
+        dz=vm((all_rows, width), BF),
+        dh=vm((all_rows, width), BF),
+        dy=vm((own_rows, width), F32),
+        dqkv=vm((all_rows, 3 * hw), BF),
+        acc=vm((8, width), F32),
+        hacc=vm((8, fw), F32),
+        qacc=vm((8, hw), F32),
+        kt=vm((hw, full), BF),
+        ot=vm((hw, full), F32),
+        dk_acc=vm((full, hw), F32),
+        dv_acc=vm((full, hw), F32),
+        da=vm((full, hw), BF),
+        mixed_send=vm((own_rows, width), BF),
+        back_send=vm((own_rows, width), BF),
+        back_recv=vm((slots, rows, width), BF),
+        gs=vm((fw, width), BF),
+        gs_y=vm((fw, n_z * dw), BF),
+        gs_z=vm((fw, (n_z - 1) * dw), BF),
+        ge=vm((width, fw), BF),
+        ge_y=vm((n_z * dw, fw), BF),
+        ge_z=vm(((n_z - 1) * dw, fw), BF),
+        go=vm((hw, width), BF),
+        go_y=vm((hw, n_z * dw), BF),
+        go_z=vm((hw, (n_z - 1) * dw), BF),
+        g3=vm((width, 3 * hw), BF),
+        g3_y=vm((n_z * dw, 3 * hw), BF),
+        g3_z=vm(((n_z - 1) * dw, 3 * hw), BF),
+        small_send=vm((n_dp, 16, dw), F32),
+        small_recv=vm((n_dp, 16, dw), F32),
+        small_t=vm((n_t, 16, dw), F32),
+        send_sems=pltpu.SemaphoreType.DMA((N_SEM,)),
+        recv_sems=pltpu.SemaphoreType.DMA((N_SEM,)),
+        local_sems=pltpu.SemaphoreType.DMA((24,)),
+    )
+    g = types.SimpleNamespace(
+        n_seq=n_seq,
+        quarter=quarter,
+        width=width,
+        n_dp=n_dp,
+        n_y=n_y,
+        n_t=n_t,
+        head_width=hw,
+        hidden_width=fw,
+        ebias_rows=ebias_rows,
+        scratch_names=tuple(scratch),
+    )
+    smem = pl.BlockSpec(memory_space=pltpu.SMEM)
+    vmem = pl.BlockSpec(memory_space=pltpu.VMEM)
+    anywhere = pl.BlockSpec(memory_space=pl.ANY)
+    sds = jax.ShapeDtypeStruct
+    flops = 2 * all_rows * (3 * width * 3 * hw + 3 * width * hw + 6 * width * fw + 7 * full * hw)
+    mixed, back, g3, go, ge, gs, small = pl.pallas_call(
+        functools.partial(layer_kernel, g),
+        out_shape=(
+            sds(tokens.shape[:1] + (rows, width), BF),
+            sds(tokens.shape[:1] + (rows, width), BF),
+            sds((dw, 3 * hw), F32),
+            sds((hw, dw), F32),
+            sds((dw, fw), F32),
+            sds((fw, dw), F32),
+            sds((16, dw), F32),
+        ),
+        in_specs=[smem] * 3 + [vmem] + [anywhere] * 6,
+        out_specs=[anywhere] + [vmem] * 6,
+        scratch_shapes=list(scratch.values()),
+        compiler_params=pltpu.CompilerParams(
+            collective_id=0,
+            has_side_effects=True,
+            vmem_limit_bytes=VMEM_BYTES,
+        ),
+        cost_estimate=pl.CostEstimate(flops=flops, bytes_accessed=1 << 24, transcendentals=0),
+    )(
+        order,
+        inverse,
+        lengths,
+        tokens.reshape(slots, rows, width),
+        cotangent.reshape(slots, rows, width),
+        w3,
+        output_weight,
+        expand_weight,
+        shrink_weight,
+        pack,
+    )
+    return (
+        mixed.reshape(tokens.shape),
+        back.reshape(tokens.shape),
+        jnp.stack([g3[:, i * hw : (i + 1) * hw] for i in range(3)]),
+        go,
+        ge,
+        gs,
+        small[0:6],
+        small[6:8],
+        small[8 : 8 + ebias_rows].reshape(expand_bias.shape),
     )
 
 

time: 1090 us -> 315 us (0.29)
  waiting for transfers between devices: 716 us -> 0 us
  Pallas kernels: 0 us -> 301 us
  blocking collectives: 154 us -> 0 us
  matrix products: 85.6 us -> 0 us
  local copies, waits for them, and re-layouts: 71.8 us -> 9.65 us
  other arithmetic: 28.6 us -> 2.76 us
  between operations: 16 us -> 0.69 us
  starting transfers between devices: 14.6 us -> 0 us
    reduce_scatter x9 -> x0, waiting for transfers between devices: 448 us -> none  [the longest x1 91.9 us: body(): lax.psum_scatter(expand_grad, 'dp', scatter_dimension=0, tiled=True)]
    pallas_call x0 -> x1, Pallas kernels: none -> 301 us  [body(): pl.pallas_call(functools.partial(layer_kernel, g), out_shape=(sds(tokens....]
    all_gather x8 -> x0, waiting for transfers between devices: 224 us -> none  [the longest x1 47.7 us: body(): lax.all_gather(expand_weight, 'dp', axis=0, tiled=True)]
    dot_general x33 -> x0, matrix products: 85.6 us -> none  [the longest x1 8.36 us: body(): jnp.einsum('uqj,jt->uqt', normalized_all_rows, widen_projection, preferre...]
    all_gather x3 -> x0, blocking collectives: 69.8 us -> none  [the longest x1 26.3 us: body(): lax.all_gather(expand_bias, 'dp', axis=0, tiled=True)]
    unnamed x1 -> x0, blocking collectives: 46.7 us -> none
    all_to_all x3 -> x0, waiting for transfers between devices: 41.7 us -> none  [the longest x1 22 us: body(): lax.all_to_all(output.astype(jnp.bfloat16), 'dp', split_axis=2, concat_ax...]
    all_to_all x1 -> x0, blocking collectives: 27.2 us -> none  [body(): lax.all_to_all(tokens[inverse], 'dp', split_axis=0, concat_axis=2, tiled=...]
  transfers between devices with their start and end apart: 21 -> 0, of which waited for: 17 -> 0; matrix products, arithmetic and copies ran while one was open for 7% -> 0% of each run, Pallas kernels for 0% -> 0%
where the time goes in v1:
time: 315 us
  Pallas kernels  301 us (96%)
  local copies, waits for them, and re-layouts  9.65 us (3%)
    pallas_call x1, Pallas kernels, body(): pl.pallas_call(functools.partial(layer_kernel, g), out_shape=(sds(tokens....  301 us

profile of v1, /device:TPU:0, one launch (start us, length us, event | category | flops | bytes accessed | tf_op | source)
XLA Modules:
  0.0 314.5 jit_solution(16007094736285028123)
XLA Ops:
  0.6 0.9 slice_bitcast_fusion.5
  1.6 0.7 pad_maximum_fusion.1.refs_5_
  2.3 0.1 pad.6.clone
  2.3 0.6 copy-done.6
  2.9 0.1 copy-done.7
  3.0 0.0 copy-done.8
  3.0 0.7 maximum_maximum_fusion.refs_9_
  3.7 0.6 select_reduce_fusion.refs_1_
  4.3 301.4 %shard_map.178 = (bf16[24,16,1024]{2,1,0:T(8,128)(2,1)}, bf16[24,16,1024]{2,1,0:T(8,128)(2,1)}, f32[128,768]{1,0:T(8,128)}, f32[256,128]{1,0:T(8,128)}, f32[128,...) custom-call(s32[24]{0:T(128)} %refs_0_.1, s32[24]{0:T(128)} %select_reduce_fusion.refs_1_, s32[24]{0:T(128)} %refs_2_.1, ...), custom_call_target="tpu_custom_call" | custom-call | flops 31809601536 | bytes 16777216 | tf_op jit(solution)/shard_map/pallas_call | solution.py:1219
  305.7 0.0 copy-start.1
  305.8 1.1 slice_bitcast_fusion.2
  306.9 0.8 pad_maximum_fusion
  307.7 0.6 slice.33
  308.3 0.6 slice_bitcast_fusion.6
  308.8 0.6 slice.34
  309.4 0.9 copy.29
  310.3 0.5 copy-done
  310.8 0.9 copy.30
  311.7 0.1 copy-done.4
  311.8 0.7 copy.31
  312.5 0.0 copy-done.3
  312.5 0.8 copy.32
  313.3 0.4 copy-done.2
  313.7 0.8 copy.33
  (13 shorter events, 0.0 us)
Async XLA Ops:
  2.3 0.7 copy-start.6
  2.3 0.7 copy-start.7
  2.3 0.7 copy-start.8
  3.0 0.7 copy-start.9
  305.7 3.7 %copy-start.1 = (bf16[24,16,1024]{2,1,0:T(8,128)(2,1)S(1)}, bf16[24,16,1024]{2,1,0:T(8,128)(2,1)}, u32[]{:S(2)}) copy-start(bf16[24,16,1024]{2,1,0:T(8,128)(2,1)} %get-tuple-element.16) | copy-start | bytes 2359300
  306.9 0.8 copy-start.5
  309.4 1.4 copy-start
  310.8 1.0 copy-start.4
  310.8 1.7 copy-start.3
  312.5 1.2 copy-start.2

commit v2 on v1

--- a/solution.py
+++ b/solution.py
@@ -304,7 +304,12 @@
 F32 = jnp.float32
 MESH = pl.DeviceIdType.MESH
 LOG2E = math.log2(math.e)
-N_SEM = 320
+N_SEM = 147
+PACK, W3, WO, WE, WS = range(5)
+GS, GE, G3, GO = range(10, 14)
+TX, TU, TZ, TH, R1, R2, R3, R4 = range(20, 28)
+TOK, COT, MIX, BACK, SMALL, SMALL_T = range(30, 36)
+RIGHT, LEFT, OVER_Y, OVER_Z, FAR, NEAR, NEAR_ON = range(40, 47)
 VMEM_BYTES = 64 * 1024 * 1024
 
 
@@ -330,10 +335,16 @@
         self.local_count = 0
 
     def slot(self, name):
+        if TX <= name[0] <= TH:
+            name = (TX,) + name[1:]
+        if R1 <= name[0] <= R4:
+            name = (R1,) + name[1:]
         return self.slots.setdefault(name, len(self.slots))
 
     def send(self, name, src, dst, where):
         i = self.slot(name)
+        if i in self.flying:
+            self.sent(name)
         copy = pltpu.make_async_remote_copy(
             src_ref=src,
             dst_ref=dst,
@@ -343,10 +354,10 @@
             device_id_type=MESH,
         )
         copy.start()
-        self.flying[name] = copy
+        self.flying[i] = copy
 
     def sent(self, name):
-        self.flying.pop(name).wait_send()
+        self.flying.pop(self.slot(name)).wait_send()
 
     def arrived(self, name, dst, where):
         i = self.slot(name)
@@ -359,6 +370,10 @@
             device_id_type=MESH,
         ).wait_recv()
 
+    def drain(self):
+        for copy in self.flying.values():
+            copy.wait_send()
+
     def local(self, src, dst):
         copy = pltpu.make_async_copy(src, dst, self.local_sems.at[self.local_count])
         self.local_count += 1
@@ -367,9 +382,9 @@
 
 
 def layer_kernel(g, *refs):
-    (order_s, inverse_s, lengths_s, tok, cot, w3, wo, we, ws, pack) = refs[:10]
-    (out_mixed, out_back, out_g3, out_go, out_ge, out_gs, out_small) = refs[10:17]
-    s = types.SimpleNamespace(**dict(zip(g.scratch_names, refs[17:])))
+    (order_s, lengths_s, tok, cot, w3, wo, we, ws, bias_in, gain_in, hidden_in) = refs[:11]
+    (out_mixed, back_recv, out_g3, out_go, out_ge, out_gs, out_small) = refs[11:18]
+    s = types.SimpleNamespace(**dict(zip(g.scratch_names, refs[18:])))
     n_seq, quarter, width = g.n_seq, g.quarter, g.width
     n_dp, n_y, n_t = g.n_dp, g.n_y, g.n_t
     n_z = n_dp // n_y
@@ -404,6 +419,13 @@
         return ((z + n_z - k) % n_z) * n_y + y
 
     y_peer = z * n_y + (1 - y)
+    ring = (1 - y) * z + y * (n_dp - 1 - z)
+
+    def ring_at(k):
+        r = (ring + n_dp + k) % n_dp
+        back = r // n_z
+        return ((1 - back) * r + back * (n_dp - 1 - r)) * n_y + back
+
     link = Links(s.send_sems, s.recv_sems, s.local_sems)
 
     barrier = pltpu.get_barrier_semaphore()
@@ -414,14 +436,14 @@
 
     stage, x_all, cots = s.stage, s.x_all, s.cots
     w3_all, wo_all, we_all, ws_all = s.w3_all, s.wo_all, s.we_all, s.ws_all
-    pack_all, vec, ebias = s.pack_all, s.vec, s.ebias
+    pack_own, vec, ebias = s.pack_own, s.vec, s.ebias
     qkv, att, lse, part = s.qkv, s.att, s.lse, s.part
     r_a, r_b, r_x = s.r_a, s.r_b, s.r_x
     n1, inv1, u_all, hid, slope = s.n1, s.inv1, s.u_all, s.hid, s.slope
     dz, dh, dy, dqkv = s.dz, s.dh, s.dy, s.dqkv
     acc, hacc, qacc = s.acc, s.hacc, s.qacc
     kt, ot, dk_acc, dv_acc, da = s.kt, s.ot, s.dk_acc, s.dv_acc, s.da
-    mixed_send, back_send, back_recv = s.mixed_send, s.back_send, s.back_recv
+    mixed_send, back_send = s.mixed_send, s.back_send
 
     def al(v, m):
         return pl.multiple_of(v, m)
@@ -434,10 +456,17 @@
 
 
     def permute(k, carry):
-        stage[k] = tok[inverse_s[k]]
+        arrival = jnp.int32(0)
+        for i in range(n_dp * n_seq):
+            arrival = jnp.where(order_s[i] == k, i, arrival)
+        stage[k] = tok[arrival]
         return carry
 
     lax.fori_loop(0, n_dp * n_seq, permute, 0)
+    pack_own[0:6, :] = bias_in[...].astype(F32)
+    pack_own[6:8, :] = gain_in[...].astype(F32)
+    pack_own[8 : 8 + ebias_rows, :] = hidden_in[...].astype(F32)
+    pack_own[8 + ebias_rows :, :] = jnp.zeros((16 - 8 - ebias_rows, dw), F32)
     acc[...] = jnp.zeros_like(acc)
     hacc[...] = jnp.zeros_like(hacc)
     qacc[...] = jnp.zeros_like(qacc)
@@ -449,29 +478,28 @@
     def tokens_start(j):
         for o in range(1, n_dp):
             e = dp_to(o)
-            link.send(("tok", j, o), stage.at[e * n_seq + j], x_block(j, d), {"dp": e})
+            link.send((TOK, j, o), stage.at[e * n_seq + j], x_block(j, d), {"dp": e})
         x_all[seq_rows(j, t * quarter + d * rows, rows), :] = stage[d * n_seq + j]
 
     def tokens_finish(j):
         for o in range(1, n_dp):
-            link.arrived(("tok", j, o), x_block(j, dp_from(o)), {"dp": dp_from(o)})
-            link.sent(("tok", j, o))
+            link.arrived((TOK, j, o), x_block(j, dp_from(o)), {"dp": dp_from(o)})
 
     def cot_block(src):
         return cots.at[:, pl.ds(al(src * rows, 16), rows), :]
+
+    own_copies = {}
 
     def cot_start():
         for o in range(1, n_dp):
             e = dp_to(o)
-            link.send(("cot", o), cot.at[pl.ds(e * n_seq, n_seq)], cot_block(d), {"dp": e})
-        own = link.local(cot.at[pl.ds(d * n_seq, n_seq)], cot_block(d))
-        return own
-
-    def cot_finish(own):
-        own.wait()
+            link.send((COT, o), cot.at[pl.ds(e * n_seq, n_seq)], cot_block(d), {"dp": e})
+        own_copies[COT] = link.local(cot.at[pl.ds(d * n_seq, n_seq)], cot_block(d))
+
+    def cot_finish():
+        own_copies.pop(COT).wait()
         for o in range(1, n_dp):
-            link.arrived(("cot", o), cot_block(dp_from(o)), {"dp": dp_from(o)})
-            link.sent(("cot", o))
+            link.arrived((COT, o), cot_block(dp_from(o)), {"dp": dp_from(o)})
 
     def cols(ref, e):
         return ref.at[:, pl.ds(al(e * dw, 128), dw)]
@@ -479,38 +507,37 @@
     def row_block(ref, e):
         return ref.at[pl.ds(al(e * dw, 16), dw), :]
 
+    def w3_block(e):
+        return w3_all.at[:, pl.ds(al(e * dw, 16), dw), :]
+
     gathers = {
-        "pack": (pack, lambda e: cols(pack_all, e)),
-        "w3": (w3, lambda e: row_block(w3_all, e)),
-        "wo": (wo.at[pl.ds(al(t * hw, 16), hw), :], lambda e: cols(wo_all, e)),
-        "we": (we, lambda e: row_block(we_all, e)),
-        "ws": (ws, lambda e: cols(ws_all, e)),
+        PACK: (pack_own, lambda e: cols(vec, e), n_dp // 2),
+        W3: (w3, w3_block, n_dp // 2),
+        WO: (
+            wo.at[pl.ds(al(t * hw, 16), hw), :],
+            lambda e: cols(wo_all, e),
+            n_dp // 2 - 1,
+        ),
+        WE: (we, lambda e: row_block(we_all, e), n_dp // 2),
+        WS: (ws, lambda e: cols(ws_all, e), n_dp // 2 - 1),
     }
-    own_copies = {}
 
     def gather_start(name):
-        src, block = gathers[name]
-        for k in range(1, n_z):
-            link.send((name, "z", k), src, block(d), {"dp": z_to(k)})
-        link.send((name, "y", 0), src, block(d), {"dp": y_peer})
+        src, block, _ = gathers[name]
+        link.send((name, RIGHT, 1), src, block(d), {"dp": ring_at(1)})
+        link.send((name, LEFT, 1), src, block(d), {"dp": ring_at(-1)})
         own_copies[name] = link.local(src, block(d))
 
-    def gather_forward(name, k):
-        _, block = gathers[name]
-        e = z_from(k)
-        link.arrived((name, "z", k), block(e), {"dp": e})
-        link.send((name, "y", k), block(e), block(e), {"dp": y_peer})
-
-    def gather_finish(name):
-        _, block = gathers[name]
+    def gather_step(name, way, k):
+        _, block, right = gathers[name]
+        steps, sign = (right, -1) if way == RIGHT else (n_dp - 1 - right, 1)
+        got = block(ring_at(sign * k))
+        link.arrived((name, way, k), got, {"dp": ring_at(sign)})
+        if k < steps:
+            link.send((name, way, k + 1), got, got, {"dp": ring_at(-sign)})
+
+    def gather_ready(name):
         own_copies.pop(name).wait()
-        for k in range(n_z):
-            e = ((z + n_z - k) % n_z) * n_y + (1 - y)
-            link.arrived((name, "y", k), block(e), {"dp": y_peer})
-        for k in range(1, n_z):
-            link.sent((name, "z", k))
-        for k in range(n_z):
-            link.sent((name, "y", k))
 
 
     def t_rows(j, who):
@@ -518,41 +545,37 @@
 
     def ag_start(buf, tag, j):
         own = buf.at[t_rows(j, t)]
-        link.send((tag, "far", j), own, own, {"tensor": t_far})
-        link.send((tag, "core", j), own, own, {"tensor": t_core})
+        link.send((tag, FAR, j), own, own, {"tensor": t_far})
+        link.send((tag, NEAR, j), own, own, {"tensor": t_core})
 
     def ag_forward(buf, tag, j):
         got = buf.at[t_rows(j, t_far)]
-        link.arrived((tag, "far", j), got, {"tensor": t_far})
-        link.send((tag, "fwd", j), got, got, {"tensor": t_core})
+        link.arrived((tag, FAR, j), got, {"tensor": t_far})
+        link.send((tag, NEAR_ON, j), got, got, {"tensor": t_core})
 
     def ag_finish(buf, tag, j):
-        link.arrived((tag, "core", j), buf.at[t_rows(j, t_core)], {"tensor": t_core})
-        link.arrived((tag, "fwd", j), buf.at[t_rows(j, t_diag)], {"tensor": t_core})
-        for what in ("far", "core", "fwd"):
-            link.sent((tag, what, j))
+        link.arrived((tag, NEAR, j), buf.at[t_rows(j, t_core)], {"tensor": t_core})
+        link.arrived((tag, NEAR_ON, j), buf.at[t_rows(j, t_diag)], {"tensor": t_core})
 
     def q_rows(j):
         return pl.ds(j * quarter, quarter)
 
     def rs_start_far(tag, j):
-        link.send((tag, "b", j), part.at[t_rows(j, t_diag)], r_b.at[q_rows(j)], {"tensor": t_core})
+        link.send((tag, NEAR_ON, j), part.at[t_rows(j, t_diag)], r_b.at[q_rows(j)], {"tensor": t_core})
 
     def rs_start_near(tag, j):
-        link.send((tag, "a", j), part.at[t_rows(j, t_core)], r_a.at[q_rows(j)], {"tensor": t_core})
+        link.send((tag, NEAR, j), part.at[t_rows(j, t_core)], r_a.at[q_rows(j)], {"tensor": t_core})
 
     def rs_forward(tag, j):
-        link.arrived((tag, "b", j), r_b.at[q_rows(j)], {"tensor": t_core})
+        link.arrived((tag, NEAR_ON, j), r_b.at[q_rows(j)], {"tensor": t_core})
         far = t_rows(j, t_far)
         both = part[far, :].astype(F32) + r_b[q_rows(j), :].astype(F32)
         part[far, :] = both.astype(BF)
-        link.send((tag, "x", j), part.at[far], r_x.at[q_rows(j)], {"tensor": t_far})
+        link.send((tag, FAR, j), part.at[far], r_x.at[q_rows(j)], {"tensor": t_far})
 
     def rs_finish(tag, j):
-        link.arrived((tag, "a", j), r_a.at[q_rows(j)], {"tensor": t_core})
-        link.arrived((tag, "x", j), r_x.at[q_rows(j)], {"tensor": t_far})
-        for what in ("a", "b", "x"):
-            link.sent((tag, what, j))
+        link.arrived((tag, NEAR, j), r_a.at[q_rows(j)], {"tensor": t_core})
+        link.arrived((tag, FAR, j), r_x.at[q_rows(j)], {"tensor": t_far})
 
     chunk = 32
 
@@ -572,6 +595,9 @@
         acc[row : row + 1, :] += jnp.sum(value, axis=0, keepdims=True)
 
     def two_halves(tag, j, fn):
+        if tag > R1:
+            for what in (NEAR_ON, NEAR, FAR):
+                link.sent((tag - 1, what, j))
         fn(al(j * full + (1 - x) * half, 16))
         rs_start_far(tag, j)
         fn(al(j * full + x * half, 16))
@@ -582,7 +608,6 @@
 
 
     def spread_vectors():
-        vec[...] = pack_all[...].astype(F32)
         for i in range(owners):
             e = t * owners + i
             for r in range(ebias_rows):
@@ -595,7 +620,7 @@
         at = pl.ds(j * full, full)
         for w in range(3):
             span = slice(w * hw, (w + 1) * hw)
-            value = mm(x_all[at, :], w3_all[:, span])
+            value = mm(x_all[at, :], w3_all[w])
             if w == 0:
                 value = value + vec[0:1, pl.ds(al(t * hw, 128), hw)]
             if w == 2:
@@ -639,7 +664,7 @@
 
             by_tiles(width, go)
 
-        two_halves("r1", j, part_rows)
+        two_halves(R1, j, part_rows)
 
     def norm_first(j):
         def go(r):
@@ -676,7 +701,7 @@
 
             by_tiles(width, go)
 
-        two_halves("r2", j, part_rows)
+        two_halves(R2, j, part_rows)
 
     def norm_second(j):
         length = lengths_s[d * n_seq + j]
@@ -689,7 +714,7 @@
             center = total - jnp.mean(total, axis=-1, keepdims=True)
             inv = lax.rsqrt(jnp.mean(center * center, axis=-1, keepdims=True) + EPSILON)
             scaled = center * inv
-            mixed_send[buf, :] = (scaled * vec[7:8, :] + vec[5:6, :]).astype(BF)
+            mixed_send[j, pl.ds(al(r, 16), chunk), :] = (scaled * vec[7:8, :] + vec[5:6, :]).astype(BF)
             place = t * quarter + r + lax.broadcasted_iota(jnp.int32, (chunk, 1), 0)
             valid = (place < length).astype(F32)
             e = cots[j, pl.ds(al(r, 16), chunk), :].astype(F32) * valid
@@ -705,25 +730,25 @@
 
         row_loop(go)
 
-    def rows_out(tag, j, src, dst):
+    def rows_out(tag, j, count, src, dst):
         for o in range(1, n_dp):
             e = dp_to(o)
             link.send(
                 (tag, j, o),
-                src.at[pl.ds(al(j * quarter + e * rows, 16), rows)],
-                dst.at[d * n_seq + j],
+                src.at[pl.ds(j, count), pl.ds(al(e * rows, 16), rows)],
+                dst.at[pl.ds(d * n_seq + j, count)],
                 {"dp": e},
             )
-        return link.local(
-            src.at[pl.ds(al(j * quarter + d * rows, 16), rows)], dst.at[d * n_seq + j]
+        own_copies[tag, j] = link.local(
+            src.at[pl.ds(j, count), pl.ds(al(d * rows, 16), rows)],
+            dst.at[pl.ds(d * n_seq + j, count)],
         )
 
-    def rows_in(tag, j, dst, own):
-        own.wait()
+    def rows_in(tag, j, count, dst):
+        own_copies.pop((tag, j)).wait()
         for o in range(1, n_dp):
             e = dp_from(o)
-            link.arrived((tag, j, o), dst.at[e * n_seq + j], {"dp": e})
-            link.sent((tag, j, o))
+            link.arrived((tag, j, o), dst.at[pl.ds(e * n_seq + j, count)], {"dp": e})
 
 
     def widen_back(j):
@@ -746,7 +771,7 @@
 
             by_tiles(width, go)
 
-        two_halves("r3", j, part_rows)
+        two_halves(R3, j, part_rows)
 
     def norm_first_back(j):
         def go(r):
@@ -800,81 +825,66 @@
     def token_rows(j):
         def part_rows(start):
             def go(n):
-                part[pl.ds(start, half), pl.ds(n, tile)] = mm_t(
-                    dqkv[pl.ds(start, half), :], w3_all[pl.ds(n, tile), :]
-                ).astype(BF)
+                total = None
+                for w in range(3):
+                    term = mm_t(
+                        dqkv[pl.ds(start, half), w * hw : (w + 1) * hw],
+                        w3_all[w, pl.ds(n, tile), :],
+                    )
+                    total = term if total is None else total + term
+                part[pl.ds(start, half), pl.ds(n, tile)] = total.astype(BF)
 
             by_tiles(width, go)
 
-        two_halves("r4", j, part_rows)
+        two_halves(R4, j, part_rows)
 
     def finish_rows(j):
         def go(r):
             buf = pl.ds(al(j * quarter + r, 16), chunk)
-            back_send[buf, :] = (dy[buf, :] + summed(j, r)).astype(BF)
+            back_send[j, pl.ds(al(r, 16), chunk), :] = (dy[buf, :] + summed(j, r)).astype(BF)
 
         row_loop(go)
 
 
-    def weight_grad(dst, left, right):
-        n = dst.shape[0]
-
-        def go(m):
-            dst[pl.ds(m, tile), :] = t_mm(left[:, pl.ds(m, tile)], right[...]).astype(BF)
-
-        by_tiles(n, go)
-
     grads = {
-        "gs": (s.gs, s.gs_y, s.gs_z, False, out_gs),
-        "ge": (s.ge, s.ge_y, s.ge_z, True, out_ge),
-        "go": (s.go, s.go_y, s.go_z, False, out_go),
-        "g3": (s.g3, s.g3_y, s.g3_z, True, out_g3),
+        GS: (dz, hid, s.gs, s.gs_y, s.gs_z, out_gs),
+        GE: (u_all, slope, s.ge, s.ge_y, s.ge_z, out_ge),
+        GO: (dh, att, s.go, s.go_y, s.go_z, out_go),
+        G3: (x_all, dqkv, s.g3, s.g3_y, s.g3_z, out_g3),
     }
 
-    def part_of(ref, by_rows, i):
-        if by_rows:
-            return (pl.ds(al(i * dw, 16), dw), slice(None))
-        return (slice(None), pl.ds(al(i * dw, 128), dw))
-
-    def grad_start(name):
-        whole, from_y, _, by_rows, _ = grads[name]
-        for k in list(range(1, n_z)) + [0]:
-            owner = ((z + k) % n_z) * n_y + (1 - y)
-            link.send(
-                (name, "y", k),
-                whole.at[part_of(whole, by_rows, owner)],
-                from_y.at[part_of(from_y, by_rows, k)],
-                {"dp": y_peer},
-            )
-
-    def grad_forward(name):
-        whole, from_y, from_z, by_rows, _ = grads[name]
-        for k in list(range(1, n_z)) + [0]:
-            mid = part_of(from_y, by_rows, k)
-            link.arrived((name, "y", k), from_y.at[mid], {"dp": y_peer})
-            owner = ((z + k) % n_z) * n_y + y
-            both = whole[part_of(whole, by_rows, owner)].astype(F32) + from_y[mid].astype(F32)
-            from_y[mid] = both.astype(BF)
-            if k:
-                link.send(
-                    (name, "z", k),
-                    from_y.at[mid],
-                    from_z.at[part_of(from_z, by_rows, k - 1)],
-                    {"dp": z_to(k)},
-                )
+    def owned(i):
+        return pl.ds(al(i * dw, 16), dw)
+
+    def grad_tile(name, k):
+        left, right, whole, from_y, _, _ = grads[name]
+        first = ((z + k) % n_z) * n_y
+        both = pl.ds(al(first * dw, n_y * dw), n_y * dw)
+        whole[both, :] = t_mm(left[:, both], right[...]).astype(BF)
+        link.send(
+            (name, OVER_Y, k),
+            whole.at[owned(first + (1 - y))],
+            from_y.at[owned(k)],
+            {"dp": y_peer},
+        )
+
+    def grad_forward(name, k):
+        _, _, whole, from_y, from_z, _ = grads[name]
+        mid = from_y.at[owned(k)]
+        link.arrived((name, OVER_Y, k), mid, {"dp": y_peer})
+        owner = ((z + k) % n_z) * n_y + y
+        pair = whole[owned(owner), :].astype(F32) + from_y[owned(k), :].astype(F32)
+        from_y[owned(k), :] = pair.astype(BF)
+        if k:
+            link.send((name, OVER_Z, k), mid, from_z.at[owned(k - 1)], {"dp": z_to(k)})
 
     def grad_finish(name):
-        _, from_y, from_z, by_rows, out = grads[name]
-        total = from_y[part_of(from_y, by_rows, 0)].astype(F32)
+        _, _, _, from_y, from_z, out = grads[name]
+        total = from_y[owned(0), :].astype(F32)
         for k in range(1, n_z):
-            at = part_of(from_z, by_rows, k - 1)
-            link.arrived((name, "z", k), from_z.at[at], {"dp": z_from(k)})
-            total = total + from_z[at].astype(F32)
+            link.arrived((name, OVER_Z, k), from_z.at[owned(k - 1)], {"dp": z_from(k)})
+            total = total + from_z[owned(k - 1), :].astype(F32)
         out[...] = total
-        for k in range(1, n_z):
-            link.sent((name, "z", k))
-        for k in range(n_z):
-            link.sent((name, "y", k))
 
     small_send, small_recv, small_t = s.small_send, s.small_recv, s.small_t
 
@@ -890,193 +900,264 @@
                 small_send[e, 8 + r : 9 + r, :] = hacc[0:1, at : at + dw]
         for o in range(1, n_dp):
             e = dp_to(o)
-            link.send(("small", o), small_send.at[e], small_recv.at[o], {"dp": e})
+            link.send((SMALL, o), small_send.at[e], small_recv.at[o], {"dp": e})
 
     def small_forward():
         total = small_send[d]
         for o in range(1, n_dp):
-            link.arrived(("small", o), small_recv.at[o], {"dp": dp_from(o)})
+            link.arrived((SMALL, o), small_recv.at[o], {"dp": dp_from(o)})
             total = total + small_recv[o]
-            link.sent(("small", o))
         small_t[t] = total
-        for what, peer in (("c", t_core), ("f", t_far), ("g", t_diag)):
-            link.send(("small_t", what), small_t.at[t], small_t.at[t], {"tensor": peer})
+        for what, peer in ((NEAR, t_core), (FAR, t_far), (NEAR_ON, t_diag)):
+            link.send((SMALL_T, what), small_t.at[t], small_t.at[t], {"tensor": peer})
 
     def small_finish():
-        for what, peer in (("c", t_core), ("f", t_far), ("g", t_diag)):
-            link.arrived(("small_t", what), small_t.at[peer], {"tensor": peer})
-            link.sent(("small_t", what))
+        for what, peer in ((NEAR, t_core), (FAR, t_far), (NEAR_ON, t_diag)):
+            link.arrived((SMALL_T, what), small_t.at[peer], {"tensor": peer})
         total = small_t[0]
         for i in range(1, n_t):
             total = total + small_t[i]
         out_small[...] = total
 
 
-    def reduce_pair(tag, j):
-        rs_finish(tag, j)
-
-    seqs = range(n_seq)
-    last = n_seq - 1
+    gather_start(W3)
+    gather_start(PACK)
+    tokens_start(2)
+    gather_start(WO)
+    gather_step(PACK, RIGHT, 1)
+    gather_step(W3, RIGHT, 1)
+    gather_step(W3, LEFT, 1)
+    gather_step(PACK, RIGHT, 2)
+    gather_step(PACK, LEFT, 1)
+    tokens_finish(2)
+    ag_start(x_all, TX, 2)
+    gather_step(WO, LEFT, 1)
+    tokens_start(1)
+    gather_step(W3, RIGHT, 2)
+    gather_step(PACK, LEFT, 2)
     tokens_start(0)
-    gather_start("pack")
-    gather_start("w3")
-    for j in seqs[1:]:
-        tokens_start(j)
-    gather_start("wo")
+    gather_step(PACK, RIGHT, 3)
+    gather_step(WO, LEFT, 2)
+    tokens_finish(1)
+    ag_start(x_all, TX, 1)
+    gather_step(WO, RIGHT, 1)
+    gather_step(W3, LEFT, 2)
+    gather_step(W3, RIGHT, 3)
+    ag_forward(x_all, TX, 2)
+    gather_step(PACK, LEFT, 3)
+    gather_step(PACK, RIGHT, 4)
+    ag_finish(x_all, TX, 2)
+    gather_step(WO, LEFT, 3)
     tokens_finish(0)
-    ag_start(x_all, "x", 0)
-    for k in range(1, n_z):
-        gather_forward("pack", k)
-        gather_forward("w3", k)
-    for j in seqs[1:]:
-        tokens_finish(j)
-        ag_start(x_all, "x", j)
-    for k in range(1, n_z):
-        gather_forward("wo", k)
-    for j in seqs:
-        ag_forward(x_all, "x", j)
-    gather_finish("pack")
+    ag_start(x_all, TX, 0)
+    ag_forward(x_all, TX, 1)
+    gather_step(WO, RIGHT, 2)
+    gather_start(WE)
+    ag_finish(x_all, TX, 1)
+    gather_step(W3, LEFT, 3)
+    gather_step(W3, RIGHT, 4)
+    gather_ready(PACK)
     spread_vectors()
-    gather_finish("w3")
-    gather_start("we")
-    gather_start("ws")
-    ag_finish(x_all, "x", 0)
+    gather_ready(W3)
+    gather_step(WO, LEFT, 4)
+    project(2)
+    attention(2)
+    gather_step(WO, RIGHT, 3)
+    project(1)
+    gather_start(WS)
+    ag_forward(x_all, TX, 0)
+    gather_ready(WO)
+    project_out(2)
+    gather_step(WE, RIGHT, 1)
+    ag_finish(x_all, TX, 0)
+    gather_step(WE, LEFT, 1)
+    rs_forward(R1, 2)
+    attention(1)
+    project_out(1)
+    rs_forward(R1, 1)
+    gather_step(WS, LEFT, 1)
     project(0)
+    gather_step(WS, RIGHT, 1)
     attention(0)
-    for k in range(1, n_z):
-        gather_forward("we", k)
-    gather_finish("wo")
+    gather_step(WE, LEFT, 2)
+    rs_finish(R1, 2)
+    norm_first(2)
+    ag_start(u_all, TU, 2)
+    gather_step(WE, RIGHT, 2)
+    rs_finish(R1, 1)
+    norm_first(1)
+    ag_start(u_all, TU, 1)
+    gather_step(WS, LEFT, 2)
     project_out(0)
-    ag_finish(x_all, "x", 1)
-    project(1)
-    rs_forward("r1", 0)
-    attention(1)
-    for k in range(1, n_z):
-        gather_forward("ws", k)
-    cot_own = cot_start()
-    project_out(1)
-    rs_finish("r1", 0)
+    gather_step(WE, RIGHT, 3)
+    gather_step(WE, LEFT, 3)
+    ag_forward(u_all, TU, 2)
+    rs_forward(R1, 0)
+    ag_forward(u_all, TU, 1)
+    ag_finish(u_all, TU, 1)
+    gather_step(WS, LEFT, 3)
+    gather_step(WS, RIGHT, 2)
+    gather_step(WE, RIGHT, 4)
+    gather_ready(WE)
+    widen(1)
+    ag_finish(u_all, TU, 2)
+    rs_finish(R1, 0)
     norm_first(0)
-    ag_start(u_all, "u", 0)
-    ag_finish(x_all, "x", 2)
-    project(2)
-    rs_forward("r1", 1)
-    attention(2)
-    ag_forward(u_all, "u", 0)
-    project_out(2)
-    rs_finish("r1", 1)
-    norm_first(1)
-    ag_start(u_all, "u", 1)
-    gather_finish("we")
-    ag_finish(u_all, "u", 0)
-    rs_forward("r1", 2)
+    ag_start(u_all, TU, 0)
+    widen(2)
+    cot_start()
+    gather_step(WS, RIGHT, 3)
+    gather_step(WS, LEFT, 4)
+    gather_ready(WS)
+    shrink_rows(1)
+    rs_forward(R2, 1)
+    shrink_rows(2)
+    ag_forward(u_all, TU, 0)
+    rs_forward(R2, 2)
+    ag_finish(u_all, TU, 0)
     widen(0)
-    ag_forward(u_all, "u", 1)
-    gather_finish("ws")
     shrink_rows(0)
-    rs_finish("r1", 2)
-    norm_first(2)
-    ag_start(u_all, "u", 2)
-    ag_finish(u_all, "u", 1)
-    rs_forward("r2", 0)
-    widen(1)
-    ag_forward(u_all, "u", 2)
-    cot_finish(cot_own)
-    shrink_rows(1)
-    mixed_own = []
-    rs_finish("r2", 0)
+    rs_forward(R2, 0)
+    cot_finish()
+    rs_finish(R2, 2)
+    norm_second(2)
+    ag_start(dz, TZ, 2)
+    rs_finish(R2, 0)
     norm_second(0)
-    ag_start(dz, "z", 0)
-    ag_finish(u_all, "u", 2)
-    rs_forward("r2", 1)
-    widen(2)
-    ag_forward(dz, "z", 0)
-    shrink_rows(2)
-    rs_finish("r2", 1)
+    ag_start(dz, TZ, 0)
+    ag_forward(dz, TZ, 2)
+    rs_finish(R2, 1)
     norm_second(1)
-    ag_start(dz, "z", 1)
-    ag_finish(dz, "z", 0)
-    rs_forward("r2", 2)
+    ag_start(dz, TZ, 1)
+    rows_out(MIX, 0, n_seq, mixed_send, out_mixed)
+    ag_finish(dz, TZ, 2)
+    widen_back(2)
+    ag_forward(dz, TZ, 0)
+    normed_rows(2)
+    rs_forward(R3, 2)
+    ag_forward(dz, TZ, 1)
+    ag_finish(dz, TZ, 1)
+    ag_finish(dz, TZ, 0)
+    grad_tile(GS, 1)
     widen_back(0)
-    ag_forward(dz, "z", 1)
+    widen_back(1)
+    rs_finish(R3, 2)
+    norm_first_back(2)
+    ag_start(dh, TH, 2)
+    grad_tile(GS, 2)
+    grad_forward(GS, 1)
     normed_rows(0)
-    rs_finish("r2", 2)
-    norm_second(2)
-    ag_start(dz, "z", 2)
-    for j in seqs:
-        mixed_own.append(rows_out("mix", j, mixed_send, out_mixed))
-    ag_finish(dz, "z", 1)
-    rs_forward("r3", 0)
-    widen_back(1)
-    ag_forward(dz, "z", 2)
+    rs_forward(R3, 0)
+    grad_tile(GS, 3)
+    grad_forward(GS, 2)
     normed_rows(1)
-    rs_finish("r3", 0)
+    grad_tile(GE, 1)
+    grad_forward(GS, 3)
+    grad_tile(GE, 2)
+    ag_forward(dh, TH, 2)
+    rs_finish(R3, 0)
     norm_first_back(0)
-    ag_start(dh, "h", 0)
-    ag_finish(dz, "z", 2)
-    rs_forward("r3", 1)
-    widen_back(2)
-    ag_forward(dh, "h", 0)
-    normed_rows(2)
-    rs_finish("r3", 1)
+    ag_start(dh, TH, 0)
+    ag_finish(dh, TH, 2)
+    rs_forward(R3, 1)
+    attention_back(2)
+    grad_forward(GE, 1)
+    grad_tile(GS, 0)
+    token_rows(2)
+    ag_forward(dh, TH, 0)
+    grad_tile(GE, 3)
+    ag_finish(dh, TH, 0)
+    rs_finish(R3, 1)
     norm_first_back(1)
-    ag_start(dh, "h", 1)
-    weight_grad(s.gs, hid, dz)
-    grad_start("gs")
-    rs_forward("r3", 2)
-    ag_forward(dh, "h", 1)
-    ag_finish(dh, "h", 0)
+    ag_start(dh, TH, 1)
+    grad_forward(GE, 2)
+    grad_forward(GS, 0)
+    grad_tile(GE, 0)
+    rs_forward(R4, 2)
     attention_back(0)
-    rs_finish("r3", 2)
-    norm_first_back(2)
-    ag_start(dh, "h", 2)
+    grad_forward(GE, 3)
+    ag_forward(dh, TH, 1)
+    ag_finish(dh, TH, 1)
+    grad_tile(GO, 1)
     token_rows(0)
-    grad_forward("gs")
-    weight_grad(s.ge, u_all, slope)
-    grad_start("ge")
-    rs_forward("r4", 0)
-    ag_forward(dh, "h", 2)
-    ag_finish(dh, "h", 1)
+    grad_tile(GO, 2)
+    grad_tile(GO, 3)
+    grad_finish(GS)
+    rs_forward(R4, 0)
+    rs_finish(R4, 2)
+    finish_rows(2)
+    rows_out(BACK, 2, 1, back_send, back_recv)
+    rows_in(MIX, 0, n_seq, out_mixed)
     attention_back(1)
-    rs_finish("r4", 0)
+    grad_forward(GE, 0)
+    grad_forward(GO, 3)
+    grad_tile(GO, 0)
+    grad_tile(G3, 1)
+    grad_forward(GO, 2)
+    grad_tile(G3, 2)
+    small_start()
+    rs_finish(R4, 0)
     finish_rows(0)
-    back_own = [rows_out("back", 0, back_send, back_recv)]
+    rows_out(BACK, 0, 1, back_send, back_recv)
+    small_forward()
+    grad_forward(GO, 1)
+    small_finish()
+    grad_forward(G3, 1)
+    grad_tile(G3, 3)
     token_rows(1)
-    grad_forward("ge")
-    ag_finish(dh, "h", 2)
-    rs_forward("r4", 1)
-    attention_back(2)
-    weight_grad(s.g3, x_all, dqkv)
-    grad_start("g3")
-    token_rows(2)
-    rs_finish("r4", 1)
+    grad_forward(G3, 2)
+    grad_forward(GO, 0)
+    rs_forward(R4, 1)
+    grad_forward(G3, 3)
+    grad_finish(GO)
+    rows_in(BACK, 2, 1, back_recv)
+    rows_in(BACK, 0, 1, back_recv)
+    grad_tile(G3, 0)
+    grad_finish(GE)
+    rs_finish(R4, 1)
     finish_rows(1)
-    back_own.append(rows_out("back", 1, back_send, back_recv))
-    rs_forward("r4", 2)
-    grad_forward("g3")
-    small_start()
-    weight_grad(s.go, att, dh)
-    grad_start("go")
-    rs_finish("r4", 2)
-    finish_rows(2)
-    back_own.append(rows_out("back", 2, back_send, back_recv))
-    grad_finish("gs")
-    grad_finish("ge")
-    for j in seqs:
-        rows_in("mix", j, out_mixed, mixed_own[j])
-    small_forward()
-    grad_forward("go")
-    grad_finish("g3")
-    small_finish()
-    grad_finish("go")
-    for j in seqs:
-        rows_in("back", j, back_recv, back_own[j])
-
-    def restore(k, carry):
-        out_back[k] = back_recv[order_s[k]]
+    rows_out(BACK, 1, 1, back_send, back_recv)
+    grad_forward(G3, 0)
+    grad_finish(G3)
+    rows_in(BACK, 1, 1, back_recv)
+    link.drain()
+
+
+def finish_kernel(
+    ebias_rows,
+    order_s,
+    mixed,
+    back,
+    g3,
+    go,
+    ge,
+    gs,
+    small,
+    out_mixed,
+    out_back,
+    out_g3,
+    out_go,
+    out_ge,
+    out_gs,
+    out_biases,
+    out_gains,
+    out_hidden,
+):
+    def move(k, carry):
+        out_back[k] = back[order_s[k]]
         return carry
 
-    lax.fori_loop(0, n_dp * n_seq, restore, 0)
+    lax.fori_loop(0, out_back.shape[0], move, 0)
+    out_mixed[...] = mixed[...]
+    width = out_g3.shape[2]
+    for w in range(3):
+        out_g3[w] = g3[:, w * width : (w + 1) * width]
+    out_go[...] = jnp.transpose(go[...])
+    out_gs[...] = jnp.transpose(gs[...])
+    out_ge[...] = ge[...]
+    out_biases[...] = small[0:6]
+    out_gains[...] = small[6:8]
+    out_hidden[...] = small[8 : 8 + ebias_rows]
 
 
 def body(
@@ -1127,18 +1208,6 @@
     n_y = 2
     n_z = n_dp // n_y
     ebias_rows = expand_bias.shape[0] // dw
-    ids = jnp.arange(slots, dtype=jnp.int32)
-    inverse = jnp.sum(jnp.where(order[None, :] == ids[:, None], ids[None, :], 0), axis=1)
-    pack_rows = 16
-    pack = jnp.concatenate(
-        [
-            biases,
-            gains,
-            expand_bias.reshape(ebias_rows, dw),
-            jnp.zeros((pack_rows - 8 - ebias_rows, dw), BF),
-        ]
-    )
-    w3 = jnp.concatenate([triple_weight[0], triple_weight[1], triple_weight[2]], axis=1)
     all_rows = n_seq * full
     own_rows = n_seq * quarter
     vm = pltpu.VMEM
@@ -1146,12 +1215,12 @@
         stage=vm((slots, rows, width), BF),
         x_all=vm((all_rows, width), BF),
         cots=vm((n_seq, quarter, width), BF),
-        w3_all=vm((width, 3 * hw), BF),
+        w3_all=vm((3, width, hw), BF),
         wo_all=vm((hw, width), BF),
         we_all=vm((width, fw), BF),
         ws_all=vm((fw, width), BF),
-        pack_all=vm((pack_rows, width), BF),
-        vec=vm((pack_rows, width), F32),
+        pack_own=vm((16, dw), F32),
+        vec=vm((16, width), F32),
         ebias=vm((8, fw), F32),
         qkv=vm((all_rows, 3 * hw), BF),
         att=vm((all_rows, hw), BF),
@@ -1177,18 +1246,17 @@
         dk_acc=vm((full, hw), F32),
         dv_acc=vm((full, hw), F32),
         da=vm((full, hw), BF),
-        mixed_send=vm((own_rows, width), BF),
-        back_send=vm((own_rows, width), BF),
-        back_recv=vm((slots, rows, width), BF),
-        gs=vm((fw, width), BF),
-        gs_y=vm((fw, n_z * dw), BF),
-        gs_z=vm((fw, (n_z - 1) * dw), BF),
+        mixed_send=vm((n_seq, quarter, width), BF),
+        back_send=vm((n_seq, quarter, width), BF),
+        gs=vm((width, fw), BF),
+        gs_y=vm((n_z * dw, fw), BF),
+        gs_z=vm(((n_z - 1) * dw, fw), BF),
         ge=vm((width, fw), BF),
         ge_y=vm((n_z * dw, fw), BF),
         ge_z=vm(((n_z - 1) * dw, fw), BF),
-        go=vm((hw, width), BF),
-        go_y=vm((hw, n_z * dw), BF),
-        go_z=vm((hw, (n_z - 1) * dw), BF),
+        go=vm((width, hw), BF),
+        go_y=vm((n_z * dw, hw), BF),
+        go_z=vm(((n_z - 1) * dw, hw), BF),
         g3=vm((width, 3 * hw), BF),
         g3_y=vm((n_z * dw, 3 * hw), BF),
         g3_z=vm(((n_z - 1) * dw, 3 * hw), BF),
@@ -1222,13 +1290,13 @@
             sds(tokens.shape[:1] + (rows, width), BF),
             sds(tokens.shape[:1] + (rows, width), BF),
             sds((dw, 3 * hw), F32),
-            sds((hw, dw), F32),
+            sds((dw, hw), F32),
             sds((dw, fw), F32),
-            sds((fw, dw), F32),
+            sds((dw, fw), F32),
             sds((16, dw), F32),
         ),
-        in_specs=[smem] * 3 + [vmem] + [anywhere] * 6,
-        out_specs=[anywhere] + [vmem] * 6,
+        in_specs=[smem] * 2 + [vmem] + [anywhere] * 5 + [vmem] * 3,
+        out_specs=[anywhere] * 2 + [vmem] * 5,
         scratch_shapes=list(scratch.values()),
         compiler_params=pltpu.CompilerParams(
             collective_id=0,
@@ -1238,26 +1306,39 @@
         cost_estimate=pl.CostEstimate(flops=flops, bytes_accessed=1 << 24, transcendentals=0),
     )(
         order,
-        inverse,
         lengths,
         tokens.reshape(slots, rows, width),
         cotangent.reshape(slots, rows, width),
-        w3,
+        triple_weight,
         output_weight,
         expand_weight,
         shrink_weight,
-        pack,
-    )
+        biases,
+        gains,
+        expand_bias.reshape(ebias_rows, dw),
+    )
+    finals = pl.pallas_call(
+        functools.partial(finish_kernel, ebias_rows),
+        out_shape=(
+            sds(mixed.shape, BF),
+            sds(back.shape, BF),
+            sds((3, dw, hw), F32),
+            sds((hw, dw), F32),
+            sds((dw, fw), F32),
+            sds((fw, dw), F32),
+            sds((6, dw), F32),
+            sds((2, dw), F32),
+            sds((ebias_rows, dw), F32),
+        ),
+        in_specs=[smem] + [vmem] * 7,
+        out_specs=[vmem] * 9,
+        compiler_params=pltpu.CompilerParams(vmem_limit_bytes=VMEM_BYTES),
+    )(order, mixed, back, g3, go, ge, gs, small)
     return (
-        mixed.reshape(tokens.shape),
-        back.reshape(tokens.shape),
-        jnp.stack([g3[:, i * hw : (i + 1) * hw] for i in range(3)]),
-        go,
-        ge,
-        gs,
-        small[0:6],
-        small[6:8],
-        small[8 : 8 + ebias_rows].reshape(expand_bias.shape),
+        finals[0].reshape(tokens.shape),
+        finals[1].reshape(tokens.shape),
+        *finals[2:8],
+        finals[8].reshape(expand_bias.shape),
     )
 
 

time: 315 us -> 240 us (0.76)
  Pallas kernels: 301 us -> 239 us
  local copies, waits for them, and re-layouts: 9.65 us -> 0 us
    pallas_call x1, Pallas kernels: 301 us -> 235 us  [body(): pl.pallas_call(functools.partial(layer_kernel, g), out_shape=(sds(tokens....]
    unnamed x25 -> x0, local copies, waits for them, and re-layouts: 5.79 us -> none
    pallas_call x0 -> x1, Pallas kernels: none -> 3.69 us  [body(): pl.pallas_call(functools.partial(finish_kernel, ebias_rows), out_shape=(s...]
where the time goes in v2:
time: 240 us
  Pallas kernels  239 us (100%)
    pallas_call x1, Pallas kernels, body(): pl.pallas_call(functools.partial(layer_kernel, g), out_shape=(sds(tokens....  235 us

profile of v2, /device:TPU:0, one launch (start us, length us, event | category | flops | bytes accessed | tf_op | source)
XLA Modules:
  0.0 239.5 jit_solution(1715365132301146675)
XLA Ops:
  0.6 235.2 %shard_map.178 = (bf16[24,16,1024]{2,1,0:T(8,128)(2,1)}, bf16[24,16,1024]{2,1,0:T(8,128)(2,1)}, f32[128,768]{1,0:T(8,128)}, f32[128,256]{1,0:T(8,128)}, f32[128,...) custom-call(s32[24]{0:T(128)} %order_s.1, s32[24]{0:T(128)} %refs_1_.1, bf16[24,16,1024]{2,1,0:T(8,128)(2,1)} %bitcast.10, ...), custom_call_target="tpu_custom_call" | custom-call | flops 31809601536 | bytes 16777216 | tf_op jit(solution)/shard_map/pallas_call | solution.py:1287
  235.8 3.7 %shard_map.179 = (bf16[24,16,1024]{2,1,0:T(8,128)(2,1)}, bf16[24,16,1024]{2,1,0:T(8,128)(2,1)}, f32[3,128,256]{2,1,0:T(8,128)}, f32[256,128]{1,0:T(8,128)}, f32[...) custom-call(s32[24]{0:T(128)} %order_s.1, ...), custom_call_target="tpu_custom_call" | custom-call | tf_op jit(solution)/shard_map/pallas_call | solution.py:1320

commit v3 on v2

--- a/solution.py
+++ b/solution.py
@@ -869,22 +869,19 @@
         )
 
     def grad_forward(name, k):
-        _, _, whole, from_y, from_z, _ = grads[name]
+        _, _, whole, from_y, from_z, out = grads[name]
         mid = from_y.at[owned(k)]
         link.arrived((name, OVER_Y, k), mid, {"dp": y_peer})
         owner = ((z + k) % n_z) * n_y + y
-        pair = whole[owned(owner), :].astype(F32) + from_y[owned(k), :].astype(F32)
-        from_y[owned(k), :] = pair.astype(BF)
+        total = whole[owned(owner), :].astype(F32) + from_y[owned(k), :].astype(F32)
+        if k < n_z - 1:
+            link.arrived((name, OVER_Z, k + 1), from_z.at[owned(k)], {"dp": z_from(1)})
+            total = total + from_z[owned(k), :].astype(F32)
         if k:
-            link.send((name, OVER_Z, k), mid, from_z.at[owned(k - 1)], {"dp": z_to(k)})
-
-    def grad_finish(name):
-        _, _, _, from_y, from_z, out = grads[name]
-        total = from_y[owned(0), :].astype(F32)
-        for k in range(1, n_z):
-            link.arrived((name, OVER_Z, k), from_z.at[owned(k - 1)], {"dp": z_from(k)})
-            total = total + from_z[owned(k - 1), :].astype(F32)
-        out[...] = total
+            from_y[owned(k), :] = total.astype(BF)
+            link.send((name, OVER_Z, k), mid, from_z.at[owned(k - 1)], {"dp": z_to(1)})
+        else:
+            out[...] = total
 
     small_send, small_recv, small_t = s.small_send, s.small_recv, s.small_t
 
@@ -920,205 +917,201 @@
         out_small[...] = total
 
 
+    tokens_start(0)
+    tokens_start(1)
+    tokens_start(2)
     gather_start(W3)
+    gather_start(WO)
     gather_start(PACK)
-    tokens_start(2)
-    gather_start(WO)
+    gather_step(W3, RIGHT, 1)
+    gather_step(WO, LEFT, 1)
+    tokens_finish(0)
+    ag_start(x_all, TX, 0)
+    tokens_finish(1)
+    ag_start(x_all, TX, 1)
+    gather_step(PACK, LEFT, 1)
+    gather_step(W3, LEFT, 1)
     gather_step(PACK, RIGHT, 1)
-    gather_step(W3, RIGHT, 1)
-    gather_step(W3, LEFT, 1)
+    gather_step(PACK, LEFT, 2)
+    gather_step(WO, RIGHT, 1)
     gather_step(PACK, RIGHT, 2)
-    gather_step(PACK, LEFT, 1)
+    gather_step(W3, RIGHT, 2)
+    gather_step(WO, LEFT, 2)
+    gather_step(PACK, RIGHT, 3)
+    gather_step(W3, LEFT, 2)
+    gather_step(WO, LEFT, 3)
+    gather_step(WO, RIGHT, 2)
+    gather_step(W3, RIGHT, 3)
+    ag_forward(x_all, TX, 1)
+    gather_step(WO, RIGHT, 3)
+    gather_start(WE)
+    gather_step(PACK, RIGHT, 4)
+    ag_forward(x_all, TX, 0)
     tokens_finish(2)
     ag_start(x_all, TX, 2)
-    gather_step(WO, LEFT, 1)
-    tokens_start(1)
-    gather_step(W3, RIGHT, 2)
-    gather_step(PACK, LEFT, 2)
-    tokens_start(0)
-    gather_step(PACK, RIGHT, 3)
-    gather_step(WO, LEFT, 2)
-    tokens_finish(1)
-    ag_start(x_all, TX, 1)
-    gather_step(WO, RIGHT, 1)
-    gather_step(W3, LEFT, 2)
-    gather_step(W3, RIGHT, 3)
-    ag_forward(x_all, TX, 2)
     gather_step(PACK, LEFT, 3)
-    gather_step(PACK, RIGHT, 4)
-    ag_finish(x_all, TX, 2)
-    gather_step(WO, LEFT, 3)
-    tokens_finish(0)
-    ag_start(x_all, TX, 0)
-    ag_forward(x_all, TX, 1)
-    gather_step(WO, RIGHT, 2)
-    gather_start(WE)
-    ag_finish(x_all, TX, 1)
     gather_step(W3, LEFT, 3)
     gather_step(W3, RIGHT, 4)
+    gather_step(WO, LEFT, 4)
+    ag_finish(x_all, TX, 1)
     gather_ready(PACK)
+    ag_finish(x_all, TX, 0)
+    gather_ready(W3)
     spread_vectors()
-    gather_ready(W3)
-    gather_step(WO, LEFT, 4)
+    gather_start(WS)
+    project(1)
+    gather_ready(WO)
+    attention(1)
+    ag_forward(x_all, TX, 2)
+    project_out(1)
+    project(0)
+    gather_step(WE, RIGHT, 1)
+    gather_step(WE, LEFT, 1)
+    ag_finish(x_all, TX, 2)
+    rs_forward(R1, 1)
+    attention(0)
+    project_out(0)
+    rs_forward(R1, 0)
+    gather_step(WS, LEFT, 1)
     project(2)
+    gather_step(WE, RIGHT, 2)
+    gather_step(WE, LEFT, 2)
     attention(2)
-    gather_step(WO, RIGHT, 3)
-    project(1)
-    gather_start(WS)
-    ag_forward(x_all, TX, 0)
-    gather_ready(WO)
+    gather_step(WS, RIGHT, 1)
+    rs_finish(R1, 1)
+    norm_first(1)
+    ag_start(u_all, TU, 1)
     project_out(2)
-    gather_step(WE, RIGHT, 1)
-    ag_finish(x_all, TX, 0)
-    gather_step(WE, LEFT, 1)
     rs_forward(R1, 2)
-    attention(1)
-    project_out(1)
-    rs_forward(R1, 1)
-    gather_step(WS, LEFT, 1)
-    project(0)
-    gather_step(WS, RIGHT, 1)
-    attention(0)
-    gather_step(WE, LEFT, 2)
+    gather_step(WS, LEFT, 2)
+    gather_step(WE, RIGHT, 3)
+    gather_step(WE, LEFT, 3)
+    rs_finish(R1, 0)
+    norm_first(0)
+    ag_start(u_all, TU, 0)
+    ag_forward(u_all, TU, 1)
+    gather_step(WS, LEFT, 3)
+    gather_step(WS, RIGHT, 2)
+    ag_finish(u_all, TU, 1)
+    gather_step(WE, RIGHT, 4)
     rs_finish(R1, 2)
     norm_first(2)
     ag_start(u_all, TU, 2)
-    gather_step(WE, RIGHT, 2)
-    rs_finish(R1, 1)
-    norm_first(1)
-    ag_start(u_all, TU, 1)
-    gather_step(WS, LEFT, 2)
-    project_out(0)
-    gather_step(WE, RIGHT, 3)
-    gather_step(WE, LEFT, 3)
-    ag_forward(u_all, TU, 2)
-    rs_forward(R1, 0)
-    ag_forward(u_all, TU, 1)
-    ag_finish(u_all, TU, 1)
-    gather_step(WS, LEFT, 3)
-    gather_step(WS, RIGHT, 2)
-    gather_step(WE, RIGHT, 4)
     gather_ready(WE)
     widen(1)
-    ag_finish(u_all, TU, 2)
-    rs_finish(R1, 0)
-    norm_first(0)
-    ag_start(u_all, TU, 0)
-    widen(2)
+    ag_forward(u_all, TU, 0)
+    gather_step(WS, LEFT, 4)
     cot_start()
     gather_step(WS, RIGHT, 3)
-    gather_step(WS, LEFT, 4)
     gather_ready(WS)
     shrink_rows(1)
+    ag_finish(u_all, TU, 0)
     rs_forward(R2, 1)
-    shrink_rows(2)
-    ag_forward(u_all, TU, 0)
-    rs_forward(R2, 2)
-    ag_finish(u_all, TU, 0)
     widen(0)
+    ag_forward(u_all, TU, 2)
     shrink_rows(0)
     rs_forward(R2, 0)
+    ag_finish(u_all, TU, 2)
+    widen(2)
+    shrink_rows(2)
+    rs_forward(R2, 2)
     cot_finish()
+    rs_finish(R2, 1)
+    norm_second(1)
+    ag_start(dz, TZ, 1)
     rs_finish(R2, 2)
     norm_second(2)
     ag_start(dz, TZ, 2)
+    ag_forward(dz, TZ, 1)
     rs_finish(R2, 0)
     norm_second(0)
     ag_start(dz, TZ, 0)
+    rows_out(MIX, 0, n_seq, mixed_send, out_mixed)
+    ag_finish(dz, TZ, 1)
+    widen_back(1)
     ag_forward(dz, TZ, 2)
-    rs_finish(R2, 1)
-    norm_second(1)
-    ag_start(dz, TZ, 1)
-    rows_out(MIX, 0, n_seq, mixed_send, out_mixed)
+    normed_rows(1)
+    rs_forward(R3, 1)
     ag_finish(dz, TZ, 2)
+    ag_forward(dz, TZ, 0)
     widen_back(2)
-    ag_forward(dz, TZ, 0)
+    ag_finish(dz, TZ, 0)
+    grad_tile(GS, 3)
+    widen_back(0)
+    rs_finish(R3, 1)
+    norm_first_back(1)
+    ag_start(dh, TH, 1)
+    grad_tile(GE, 3)
+    normed_rows(0)
+    grad_tile(GS, 2)
+    rs_forward(R3, 0)
+    grad_forward(GS, 3)
     normed_rows(2)
+    ag_forward(dh, TH, 1)
+    grad_tile(GE, 2)
+    grad_tile(GS, 1)
     rs_forward(R3, 2)
-    ag_forward(dz, TZ, 1)
-    ag_finish(dz, TZ, 1)
-    ag_finish(dz, TZ, 0)
-    grad_tile(GS, 1)
-    widen_back(0)
-    widen_back(1)
+    ag_finish(dh, TH, 1)
+    grad_forward(GE, 3)
+    attention_back(1)
+    grad_forward(GS, 2)
+    rs_finish(R3, 0)
+    norm_first_back(0)
+    ag_start(dh, TH, 0)
+    grad_tile(GE, 1)
+    token_rows(1)
+    grad_forward(GE, 2)
+    grad_tile(GS, 0)
     rs_finish(R3, 2)
     norm_first_back(2)
     ag_start(dh, TH, 2)
-    grad_tile(GS, 2)
+    ag_forward(dh, TH, 0)
+    grad_tile(GE, 0)
+    ag_finish(dh, TH, 0)
+    rs_forward(R4, 1)
     grad_forward(GS, 1)
-    normed_rows(0)
-    rs_forward(R3, 0)
-    grad_tile(GS, 3)
-    grad_forward(GS, 2)
-    normed_rows(1)
-    grad_tile(GE, 1)
-    grad_forward(GS, 3)
-    grad_tile(GE, 2)
+    attention_back(0)
+    grad_forward(GE, 1)
     ag_forward(dh, TH, 2)
-    rs_finish(R3, 0)
-    norm_first_back(0)
-    ag_start(dh, TH, 0)
+    token_rows(0)
     ag_finish(dh, TH, 2)
-    rs_forward(R3, 1)
+    grad_tile(GO, 3)
+    rs_finish(R4, 1)
+    finish_rows(1)
+    rows_out(BACK, 1, 1, back_send, back_recv)
+    rs_forward(R4, 0)
     attention_back(2)
-    grad_forward(GE, 1)
-    grad_tile(GS, 0)
+    grad_tile(G3, 3)
+    rows_in(MIX, 0, n_seq, out_mixed)
+    grad_forward(GS, 0)
+    grad_forward(GO, 3)
+    small_start()
+    grad_tile(GO, 2)
+    rs_finish(R4, 0)
+    finish_rows(0)
+    rows_out(BACK, 0, 1, back_send, back_recv)
     token_rows(2)
-    ag_forward(dh, TH, 0)
-    grad_tile(GE, 3)
-    ag_finish(dh, TH, 0)
-    rs_finish(R3, 1)
-    norm_first_back(1)
-    ag_start(dh, TH, 1)
-    grad_forward(GE, 2)
-    grad_forward(GS, 0)
-    grad_tile(GE, 0)
     rs_forward(R4, 2)
-    attention_back(0)
-    grad_forward(GE, 3)
-    ag_forward(dh, TH, 1)
-    ag_finish(dh, TH, 1)
-    grad_tile(GO, 1)
-    token_rows(0)
-    grad_tile(GO, 2)
-    grad_tile(GO, 3)
-    grad_finish(GS)
-    rs_forward(R4, 0)
+    grad_forward(GO, 2)
+    small_forward()
+    grad_forward(G3, 3)
+    grad_tile(G3, 2)
     rs_finish(R4, 2)
     finish_rows(2)
     rows_out(BACK, 2, 1, back_send, back_recv)
-    rows_in(MIX, 0, n_seq, out_mixed)
-    attention_back(1)
-    grad_forward(GE, 0)
-    grad_forward(GO, 3)
-    grad_tile(GO, 0)
+    grad_forward(G3, 2)
+    grad_tile(GO, 1)
+    rows_in(BACK, 0, 1, back_recv)
     grad_tile(G3, 1)
-    grad_forward(GO, 2)
-    grad_tile(G3, 2)
-    small_start()
-    rs_finish(R4, 0)
-    finish_rows(0)
-    rows_out(BACK, 0, 1, back_send, back_recv)
-    small_forward()
+    rows_in(BACK, 2, 1, back_recv)
+    grad_tile(G3, 0)
     grad_forward(GO, 1)
     small_finish()
+    grad_forward(GE, 0)
     grad_forward(G3, 1)
-    grad_tile(G3, 3)
-    token_rows(1)
-    grad_forward(G3, 2)
+    grad_tile(GO, 0)
     grad_forward(GO, 0)
-    rs_forward(R4, 1)
-    grad_forward(G3, 3)
-    grad_finish(GO)
-    rows_in(BACK, 2, 1, back_recv)
-    rows_in(BACK, 0, 1, back_recv)
-    grad_tile(G3, 0)
-    grad_finish(GE)
-    rs_finish(R4, 1)
-    finish_rows(1)
-    rows_out(BACK, 1, 1, back_send, back_recv)
     grad_forward(G3, 0)
-    grad_finish(G3)
     rows_in(BACK, 1, 1, back_recv)
     link.drain()
 

time: 240 us -> 229 us (0.954); the launches traced: 240 us -> 225 us
  Pallas kernels: 239 us -> 224 us
    pallas_call x1, Pallas kernels: 235 us -> 220 us  [body(): pl.pallas_call(functools.partial(layer_kernel, g), out_shape=(sds(tokens....]
where the time goes in v3:
time: 229 us; the launch traced here: 225 us
  Pallas kernels  224 us (98%)
    pallas_call x1, Pallas kernels, body(): pl.pallas_call(functools.partial(layer_kernel, g), out_shape=(sds(tokens....  220 us

profile of v3, /device:TPU:0, one launch (start us, length us, event | category | flops | bytes accessed | tf_op | source)
XLA Modules:
  0.0 224.8 jit_solution(8776752206482242365)
XLA Ops:
  0.6 220.4 %shard_map.178 = (bf16[24,16,1024]{2,1,0:T(8,128)(2,1)}, bf16[24,16,1024]{2,1,0:T(8,128)(2,1)}, f32[128,768]{1,0:T(8,128)}, f32[128,256]{1,0:T(8,128)}, f32[128,...) custom-call(s32[24]{0:T(128)} %order_s.1, s32[24]{0:T(128)} %refs_1_.1, bf16[24,16,1024]{2,1,0:T(8,128)(2,1)} %bitcast.10, ...), custom_call_target="tpu_custom_call" | custom-call | flops 31809601536 | bytes 16777216 | tf_op jit(solution)/shard_map/pallas_call | solution.py:1280
  221.1 3.7 %shard_map.179 = (bf16[24,16,1024]{2,1,0:T(8,128)(2,1)}, bf16[24,16,1024]{2,1,0:T(8,128)(2,1)}, f32[3,128,256]{2,1,0:T(8,128)}, f32[256,128]{1,0:T(8,128)}, f32[...) custom-call(s32[24]{0:T(128)} %order_s.1, ...), custom_call_target="tpu_custom_call" | custom-call | tf_op jit(solution)/shard_map/pallas_call | solution.py:1313

commit v4 on v3

--- a/solution.py
+++ b/solution.py
@@ -918,201 +918,201 @@
 
 
     tokens_start(0)
-    tokens_start(1)
-    tokens_start(2)
     gather_start(W3)
+    gather_start(PACK)
     gather_start(WO)
-    gather_start(PACK)
     gather_step(W3, RIGHT, 1)
+    gather_step(PACK, LEFT, 1)
     gather_step(WO, LEFT, 1)
+    gather_step(PACK, LEFT, 2)
     tokens_finish(0)
     ag_start(x_all, TX, 0)
+    gather_step(W3, LEFT, 1)
+    gather_step(PACK, RIGHT, 1)
+    gather_step(PACK, RIGHT, 2)
+    gather_step(WO, RIGHT, 1)
+    gather_step(WO, LEFT, 2)
+    gather_step(PACK, RIGHT, 3)
+    gather_step(W3, RIGHT, 2)
+    tokens_start(1)
+    gather_step(PACK, LEFT, 3)
+    gather_step(W3, LEFT, 2)
+    ag_forward(x_all, TX, 0)
+    gather_step(PACK, RIGHT, 4)
+    gather_step(W3, RIGHT, 3)
+    gather_step(WO, RIGHT, 2)
+    gather_ready(PACK)
+    gather_step(WO, LEFT, 3)
     tokens_finish(1)
     ag_start(x_all, TX, 1)
-    gather_step(PACK, LEFT, 1)
-    gather_step(W3, LEFT, 1)
-    gather_step(PACK, RIGHT, 1)
-    gather_step(PACK, LEFT, 2)
-    gather_step(WO, RIGHT, 1)
-    gather_step(PACK, RIGHT, 2)
-    gather_step(W3, RIGHT, 2)
-    gather_step(WO, LEFT, 2)
-    gather_step(PACK, RIGHT, 3)
-    gather_step(W3, LEFT, 2)
-    gather_step(WO, LEFT, 3)
-    gather_step(WO, RIGHT, 2)
-    gather_step(W3, RIGHT, 3)
+    gather_step(W3, LEFT, 3)
+    tokens_start(2)
+    gather_step(W3, RIGHT, 4)
+    gather_ready(W3)
+    gather_step(WO, RIGHT, 3)
     ag_forward(x_all, TX, 1)
-    gather_step(WO, RIGHT, 3)
+    ag_finish(x_all, TX, 0)
     gather_start(WE)
-    gather_step(PACK, RIGHT, 4)
-    ag_forward(x_all, TX, 0)
+    spread_vectors()
+    gather_step(WO, LEFT, 4)
+    gather_ready(WO)
+    ag_finish(x_all, TX, 1)
+    project(0)
     tokens_finish(2)
     ag_start(x_all, TX, 2)
-    gather_step(PACK, LEFT, 3)
-    gather_step(W3, LEFT, 3)
-    gather_step(W3, RIGHT, 4)
-    gather_step(WO, LEFT, 4)
-    ag_finish(x_all, TX, 1)
-    gather_ready(PACK)
-    ag_finish(x_all, TX, 0)
-    gather_ready(W3)
-    spread_vectors()
+    project(1)
     gather_start(WS)
-    project(1)
-    gather_ready(WO)
     attention(1)
+    project_out(1)
+    rs_forward(R1, 1)
+    gather_step(WE, RIGHT, 1)
     ag_forward(x_all, TX, 2)
-    project_out(1)
-    project(0)
-    gather_step(WE, RIGHT, 1)
     gather_step(WE, LEFT, 1)
-    ag_finish(x_all, TX, 2)
-    rs_forward(R1, 1)
     attention(0)
     project_out(0)
+    gather_step(WS, LEFT, 1)
+    ag_finish(x_all, TX, 2)
+    gather_step(WS, RIGHT, 1)
     rs_forward(R1, 0)
-    gather_step(WS, LEFT, 1)
-    project(2)
     gather_step(WE, RIGHT, 2)
     gather_step(WE, LEFT, 2)
-    attention(2)
-    gather_step(WS, RIGHT, 1)
     rs_finish(R1, 1)
     norm_first(1)
     ag_start(u_all, TU, 1)
+    project(2)
+    attention(2)
     project_out(2)
+    gather_step(WS, LEFT, 2)
     rs_forward(R1, 2)
-    gather_step(WS, LEFT, 2)
     gather_step(WE, RIGHT, 3)
-    gather_step(WE, LEFT, 3)
+    ag_forward(u_all, TU, 1)
     rs_finish(R1, 0)
     norm_first(0)
     ag_start(u_all, TU, 0)
-    ag_forward(u_all, TU, 1)
     gather_step(WS, LEFT, 3)
     gather_step(WS, RIGHT, 2)
+    gather_step(WE, RIGHT, 4)
+    gather_step(WE, LEFT, 3)
     ag_finish(u_all, TU, 1)
-    gather_step(WE, RIGHT, 4)
+    gather_ready(WE)
     rs_finish(R1, 2)
     norm_first(2)
     ag_start(u_all, TU, 2)
-    gather_ready(WE)
     widen(1)
     ag_forward(u_all, TU, 0)
     gather_step(WS, LEFT, 4)
-    cot_start()
     gather_step(WS, RIGHT, 3)
     gather_ready(WS)
+    cot_start()
     shrink_rows(1)
+    rs_forward(R2, 1)
     ag_finish(u_all, TU, 0)
-    rs_forward(R2, 1)
     widen(0)
     ag_forward(u_all, TU, 2)
     shrink_rows(0)
+    ag_finish(u_all, TU, 2)
     rs_forward(R2, 0)
-    ag_finish(u_all, TU, 2)
     widen(2)
     shrink_rows(2)
     rs_forward(R2, 2)
     cot_finish()
+    rs_finish(R2, 0)
+    norm_second(0)
+    ag_start(dz, TZ, 0)
+    rs_finish(R2, 2)
+    norm_second(2)
+    ag_start(dz, TZ, 2)
+    ag_forward(dz, TZ, 0)
     rs_finish(R2, 1)
     norm_second(1)
     ag_start(dz, TZ, 1)
-    rs_finish(R2, 2)
-    norm_second(2)
-    ag_start(dz, TZ, 2)
+    ag_finish(dz, TZ, 0)
+    rows_out(MIX, 0, n_seq, mixed_send, out_mixed)
+    widen_back(0)
+    ag_forward(dz, TZ, 2)
+    normed_rows(0)
+    rs_forward(R3, 0)
     ag_forward(dz, TZ, 1)
-    rs_finish(R2, 0)
-    norm_second(0)
-    ag_start(dz, TZ, 0)
-    rows_out(MIX, 0, n_seq, mixed_send, out_mixed)
+    ag_finish(dz, TZ, 2)
+    widen_back(2)
     ag_finish(dz, TZ, 1)
+    grad_tile(GS, 3)
     widen_back(1)
-    ag_forward(dz, TZ, 2)
+    rs_finish(R3, 0)
+    norm_first_back(0)
+    ag_start(dh, TH, 0)
+    grad_tile(GE, 3)
     normed_rows(1)
     rs_forward(R3, 1)
-    ag_finish(dz, TZ, 2)
-    ag_forward(dz, TZ, 0)
-    widen_back(2)
-    ag_finish(dz, TZ, 0)
-    grad_tile(GS, 3)
-    widen_back(0)
+    grad_forward(GS, 3)
+    grad_tile(GS, 2)
+    normed_rows(2)
+    ag_forward(dh, TH, 0)
+    rs_forward(R3, 2)
+    grad_forward(GE, 3)
+    grad_tile(GE, 2)
+    ag_finish(dh, TH, 0)
+    attention_back(0)
     rs_finish(R3, 1)
     norm_first_back(1)
     ag_start(dh, TH, 1)
-    grad_tile(GE, 3)
-    normed_rows(0)
-    grad_tile(GS, 2)
-    rs_forward(R3, 0)
-    grad_forward(GS, 3)
-    normed_rows(2)
-    ag_forward(dh, TH, 1)
-    grad_tile(GE, 2)
+    grad_forward(GS, 2)
     grad_tile(GS, 1)
-    rs_forward(R3, 2)
-    ag_finish(dh, TH, 1)
-    grad_forward(GE, 3)
-    attention_back(1)
-    grad_forward(GS, 2)
-    rs_finish(R3, 0)
-    norm_first_back(0)
-    ag_start(dh, TH, 0)
-    grad_tile(GE, 1)
-    token_rows(1)
     grad_forward(GE, 2)
-    grad_tile(GS, 0)
     rs_finish(R3, 2)
     norm_first_back(2)
     ag_start(dh, TH, 2)
-    ag_forward(dh, TH, 0)
-    grad_tile(GE, 0)
-    ag_finish(dh, TH, 0)
-    rs_forward(R4, 1)
+    rows_in(MIX, 0, n_seq, out_mixed)
+    grad_tile(GE, 1)
+    token_rows(0)
+    ag_forward(dh, TH, 1)
     grad_forward(GS, 1)
-    attention_back(0)
+    grad_tile(GS, 0)
+    rs_forward(R4, 0)
+    ag_forward(dh, TH, 2)
+    ag_finish(dh, TH, 1)
     grad_forward(GE, 1)
-    ag_forward(dh, TH, 2)
-    token_rows(0)
     ag_finish(dh, TH, 2)
     grad_tile(GO, 3)
+    attention_back(2)
+    rs_finish(R4, 0)
+    finish_rows(0)
+    rows_out(BACK, 0, 1, back_send, back_recv)
+    grad_forward(GO, 3)
+    grad_tile(GO, 2)
+    attention_back(1)
+    grad_tile(G3, 3)
+    token_rows(1)
+    grad_forward(GO, 2)
+    small_start()
+    rs_forward(R4, 1)
+    grad_tile(GO, 1)
+    grad_tile(G3, 2)
+    grad_forward(G3, 3)
+    token_rows(2)
+    grad_tile(G3, 1)
+    grad_forward(GO, 1)
     rs_finish(R4, 1)
     finish_rows(1)
     rows_out(BACK, 1, 1, back_send, back_recv)
-    rs_forward(R4, 0)
-    attention_back(2)
-    grad_tile(G3, 3)
-    rows_in(MIX, 0, n_seq, out_mixed)
-    grad_forward(GS, 0)
-    grad_forward(GO, 3)
-    small_start()
-    grad_tile(GO, 2)
-    rs_finish(R4, 0)
-    finish_rows(0)
-    rows_out(BACK, 0, 1, back_send, back_recv)
-    token_rows(2)
+    grad_forward(G3, 2)
+    grad_tile(GE, 0)
+    rows_in(BACK, 0, 1, back_recv)
     rs_forward(R4, 2)
-    grad_forward(GO, 2)
     small_forward()
-    grad_forward(G3, 3)
-    grad_tile(G3, 2)
+    grad_tile(GO, 0)
+    grad_tile(G3, 0)
     rs_finish(R4, 2)
     finish_rows(2)
     rows_out(BACK, 2, 1, back_send, back_recv)
-    grad_forward(G3, 2)
-    grad_tile(GO, 1)
-    rows_in(BACK, 0, 1, back_recv)
-    grad_tile(G3, 1)
-    rows_in(BACK, 2, 1, back_recv)
-    grad_tile(G3, 0)
-    grad_forward(GO, 1)
+    grad_forward(GS, 0)
+    grad_forward(G3, 1)
+    grad_forward(GO, 0)
     small_finish()
     grad_forward(GE, 0)
-    grad_forward(G3, 1)
-    grad_tile(GO, 0)
-    grad_forward(GO, 0)
+    rows_in(BACK, 1, 1, back_recv)
     grad_forward(G3, 0)
-    rows_in(BACK, 1, 1, back_recv)
+    rows_in(BACK, 2, 1, back_recv)
     link.drain()
 
 

time: 229 us -> 224 us (0.978); the launches traced: 225 us -> 224 us
  no operation moved by 1% of the time
where the time goes in v4:
time: 224 us
  Pallas kernels  224 us (100%)
    pallas_call x1, Pallas kernels, body(): pl.pallas_call(functools.partial(layer_kernel, g), out_shape=(sds(tokens....  220 us

profile of v4, /device:TPU:0, one launch (start us, length us, event | category | flops | bytes accessed | tf_op | source)
XLA Modules:
  0.0 224.3 jit_solution(13641694671832760410)
XLA Ops:
  0.6 220.0 %shard_map.178 = (bf16[24,16,1024]{2,1,0:T(8,128)(2,1)}, bf16[24,16,1024]{2,1,0:T(8,128)(2,1)}, f32[128,768]{1,0:T(8,128)}, f32[128,256]{1,0:T(8,128)}, f32[128,...) custom-call(s32[24]{0:T(128)} %order_s.1, s32[24]{0:T(128)} %refs_1_.1, bf16[24,16,1024]{2,1,0:T(8,128)(2,1)} %bitcast.10, ...), custom_call_target="tpu_custom_call" | custom-call | flops 31809601536 | bytes 16777216 | tf_op jit(solution)/shard_map/pallas_call | solution.py:1280
  220.6 3.7 %shard_map.179 = (bf16[24,16,1024]{2,1,0:T(8,128)(2,1)}, bf16[24,16,1024]{2,1,0:T(8,128)(2,1)}, f32[3,128,256]{2,1,0:T(8,128)}, f32[256,128]{1,0:T(8,128)}, f32[...) custom-call(s32[24]{0:T(128)} %order_s.1, ...), custom_call_target="tpu_custom_call" | custom-call | tf_op jit(solution)/shard_map/pallas_call | solution.py:1313

commit v5 on v4

--- a/solution.py
+++ b/solution.py
@@ -304,8 +304,8 @@
 F32 = jnp.float32
 MESH = pl.DeviceIdType.MESH
 LOG2E = math.log2(math.e)
-N_SEM = 147
-PACK, W3, WO, WE, WS = range(5)
+N_SEM = 175
+PACK, WQ, WK, WV, WO, WE0, WE1, WS0, WS1 = range(9)
 GS, GE, G3, GO = range(10, 14)
 TX, TU, TZ, TH, R1, R2, R3, R4 = range(20, 28)
 TOK, COT, MIX, BACK, SMALL, SMALL_T = range(30, 36)
@@ -504,22 +504,32 @@
     def cols(ref, e):
         return ref.at[:, pl.ds(al(e * dw, 128), dw)]
 
-    def row_block(ref, e):
-        return ref.at[pl.ds(al(e * dw, 16), dw), :]
-
-    def w3_block(e):
-        return w3_all.at[:, pl.ds(al(e * dw, 16), dw), :]
-
+    def w3_part(w, steps):
+        return (w3.at[w], lambda e: w3_all.at[w, pl.ds(al(e * dw, 16), dw), :], steps)
+
+    def we_part(i, steps):
+        span = pl.ds(i * (fw // 2), fw // 2)
+        return (we.at[:, span], lambda e: we_all.at[pl.ds(al(e * dw, 16), dw), span], steps)
+
+    def ws_part(i, steps):
+        span = pl.ds(i * (fw // 2), fw // 2)
+        return (ws.at[span, :], lambda e: ws_all.at[span, pl.ds(al(e * dw, 128), dw)], steps)
+
+    more, less = n_dp // 2, n_dp // 2 - 1
     gathers = {
         PACK: (pack_own, lambda e: cols(vec, e), n_dp // 2),
-        W3: (w3, w3_block, n_dp // 2),
+        WQ: w3_part(0, more),
+        WK: w3_part(1, less),
+        WV: w3_part(2, more),
         WO: (
             wo.at[pl.ds(al(t * hw, 16), hw), :],
             lambda e: cols(wo_all, e),
             n_dp // 2 - 1,
         ),
-        WE: (we, lambda e: row_block(we_all, e), n_dp // 2),
-        WS: (ws, lambda e: cols(ws_all, e), n_dp // 2 - 1),
+        WE0: we_part(0, more),
+        WE1: we_part(1, less),
+        WS0: ws_part(0, more),
+        WS1: ws_part(1, less),
     }
 
     def gather_start(name):
@@ -918,103 +928,139 @@
 
 
     tokens_start(0)
-    gather_start(W3)
+    gather_start(WV)
+    gather_start(WK)
+    gather_step(WV, RIGHT, 1)
+    gather_start(WQ)
+    gather_start(WO)
+    gather_step(WK, LEFT, 1)
+    gather_step(WV, RIGHT, 2)
+    gather_step(WV, LEFT, 1)
+    gather_step(WQ, RIGHT, 1)
+    gather_step(WO, LEFT, 1)
     gather_start(PACK)
-    gather_start(WO)
-    gather_step(W3, RIGHT, 1)
-    gather_step(PACK, LEFT, 1)
-    gather_step(WO, LEFT, 1)
-    gather_step(PACK, LEFT, 2)
+    tokens_start(1)
+    gather_step(WQ, LEFT, 1)
+    gather_step(WK, LEFT, 2)
+    gather_step(WV, RIGHT, 3)
+    gather_step(WK, RIGHT, 1)
+    gather_step(WQ, LEFT, 2)
+    gather_step(WO, LEFT, 2)
+    gather_step(WO, RIGHT, 1)
     tokens_finish(0)
     ag_start(x_all, TX, 0)
-    gather_step(W3, LEFT, 1)
-    gather_step(PACK, RIGHT, 1)
-    gather_step(PACK, RIGHT, 2)
-    gather_step(WO, RIGHT, 1)
-    gather_step(WO, LEFT, 2)
-    gather_step(PACK, RIGHT, 3)
-    gather_step(W3, RIGHT, 2)
-    tokens_start(1)
-    gather_step(PACK, LEFT, 3)
-    gather_step(W3, LEFT, 2)
-    ag_forward(x_all, TX, 0)
-    gather_step(PACK, RIGHT, 4)
-    gather_step(W3, RIGHT, 3)
-    gather_step(WO, RIGHT, 2)
-    gather_ready(PACK)
-    gather_step(WO, LEFT, 3)
+    gather_step(WV, RIGHT, 4)
+    tokens_start(2)
+    gather_step(WQ, RIGHT, 2)
+    gather_step(PACK, LEFT, 1)
     tokens_finish(1)
     ag_start(x_all, TX, 1)
-    gather_step(W3, LEFT, 3)
-    tokens_start(2)
-    gather_step(W3, RIGHT, 4)
-    gather_ready(W3)
+    gather_step(WQ, LEFT, 3)
+    ag_forward(x_all, TX, 0)
+    gather_step(PACK, RIGHT, 1)
+    gather_step(WO, LEFT, 3)
+    gather_step(WO, RIGHT, 2)
+    gather_step(WK, RIGHT, 2)
+    gather_step(WK, LEFT, 3)
+    gather_step(PACK, RIGHT, 2)
+    gather_step(WV, LEFT, 2)
+    ag_finish(x_all, TX, 0)
+    gather_step(WQ, RIGHT, 3)
+    gather_step(PACK, RIGHT, 3)
+    gather_step(WO, LEFT, 4)
+    gather_step(PACK, LEFT, 2)
+    gather_start(WE0)
+    tokens_finish(2)
+    ag_start(x_all, TX, 2)
     gather_step(WO, RIGHT, 3)
     ag_forward(x_all, TX, 1)
-    ag_finish(x_all, TX, 0)
-    gather_start(WE)
+    gather_ready(WO)
+    gather_start(WE1)
+    gather_start(WS1)
+    gather_step(WK, LEFT, 4)
+    gather_step(PACK, RIGHT, 4)
+    gather_step(PACK, LEFT, 3)
+    gather_ready(PACK)
+    gather_step(WV, LEFT, 3)
+    gather_step(WK, RIGHT, 3)
+    gather_ready(WK)
     spread_vectors()
-    gather_step(WO, LEFT, 4)
-    gather_ready(WO)
-    ag_finish(x_all, TX, 1)
+    gather_step(WQ, RIGHT, 4)
+    gather_ready(WV)
+    gather_ready(WQ)
     project(0)
-    tokens_finish(2)
-    ag_start(x_all, TX, 2)
-    project(1)
-    gather_start(WS)
-    attention(1)
-    project_out(1)
-    rs_forward(R1, 1)
-    gather_step(WE, RIGHT, 1)
-    ag_forward(x_all, TX, 2)
-    gather_step(WE, LEFT, 1)
     attention(0)
     project_out(0)
-    gather_step(WS, LEFT, 1)
+    ag_forward(x_all, TX, 2)
+    ag_finish(x_all, TX, 1)
+    gather_start(WS0)
+    rs_forward(R1, 0)
+    project(1)
+    gather_step(WE0, RIGHT, 1)
+    gather_step(WE0, LEFT, 1)
     ag_finish(x_all, TX, 2)
-    gather_step(WS, RIGHT, 1)
-    rs_forward(R1, 0)
-    gather_step(WE, RIGHT, 2)
-    gather_step(WE, LEFT, 2)
+    project(2)
+    attention(2)
+    gather_step(WE1, RIGHT, 1)
+    gather_step(WS1, LEFT, 1)
+    project_out(2)
+    gather_step(WS1, RIGHT, 1)
+    gather_step(WE1, LEFT, 1)
+    rs_forward(R1, 2)
+    attention(1)
+    gather_step(WS0, RIGHT, 1)
+    gather_step(WS0, LEFT, 1)
+    project_out(1)
+    gather_step(WE0, RIGHT, 2)
+    rs_forward(R1, 1)
+    gather_step(WE0, LEFT, 2)
+    gather_step(WE1, LEFT, 2)
+    rs_finish(R1, 2)
+    norm_first(2)
+    ag_start(u_all, TU, 2)
+    gather_step(WS1, LEFT, 2)
+    gather_step(WS1, RIGHT, 2)
+    gather_step(WS0, RIGHT, 2)
+    gather_step(WE1, LEFT, 3)
+    gather_step(WE1, RIGHT, 2)
+    gather_step(WS1, RIGHT, 3)
+    gather_step(WE0, RIGHT, 3)
+    rs_finish(R1, 0)
+    norm_first(0)
+    ag_start(u_all, TU, 0)
+    gather_step(WS1, LEFT, 3)
+    ag_forward(u_all, TU, 2)
+    gather_step(WS0, LEFT, 2)
+    gather_step(WS0, RIGHT, 3)
+    gather_step(WE1, RIGHT, 3)
+    gather_step(WE1, LEFT, 4)
+    ag_finish(u_all, TU, 2)
     rs_finish(R1, 1)
     norm_first(1)
     ag_start(u_all, TU, 1)
-    project(2)
-    attention(2)
-    project_out(2)
-    gather_step(WS, LEFT, 2)
-    rs_forward(R1, 2)
-    gather_step(WE, RIGHT, 3)
+    gather_step(WE0, LEFT, 3)
+    gather_step(WS1, LEFT, 4)
+    gather_step(WE0, RIGHT, 4)
+    cot_start()
+    gather_ready(WE1)
+    gather_ready(WE0)
+    widen(2)
+    ag_forward(u_all, TU, 0)
+    gather_step(WS0, LEFT, 3)
+    gather_ready(WS1)
+    gather_step(WS0, RIGHT, 4)
+    gather_ready(WS0)
+    shrink_rows(2)
+    rs_forward(R2, 2)
+    ag_finish(u_all, TU, 0)
+    widen(0)
     ag_forward(u_all, TU, 1)
-    rs_finish(R1, 0)
-    norm_first(0)
-    ag_start(u_all, TU, 0)
-    gather_step(WS, LEFT, 3)
-    gather_step(WS, RIGHT, 2)
-    gather_step(WE, RIGHT, 4)
-    gather_step(WE, LEFT, 3)
+    shrink_rows(0)
+    rs_forward(R2, 0)
     ag_finish(u_all, TU, 1)
-    gather_ready(WE)
-    rs_finish(R1, 2)
-    norm_first(2)
-    ag_start(u_all, TU, 2)
     widen(1)
-    ag_forward(u_all, TU, 0)
-    gather_step(WS, LEFT, 4)
-    gather_step(WS, RIGHT, 3)
-    gather_ready(WS)
-    cot_start()
     shrink_rows(1)
     rs_forward(R2, 1)
-    ag_finish(u_all, TU, 0)
-    widen(0)
-    ag_forward(u_all, TU, 2)
-    shrink_rows(0)
-    ag_finish(u_all, TU, 2)
-    rs_forward(R2, 0)
-    widen(2)
-    shrink_rows(2)
-    rs_forward(R2, 2)
     cot_finish()
     rs_finish(R2, 0)
     norm_second(0)
@@ -1026,93 +1072,93 @@
     rs_finish(R2, 1)
     norm_second(1)
     ag_start(dz, TZ, 1)
+    rows_out(MIX, 0, n_seq, mixed_send, out_mixed)
     ag_finish(dz, TZ, 0)
-    rows_out(MIX, 0, n_seq, mixed_send, out_mixed)
     widen_back(0)
     ag_forward(dz, TZ, 2)
     normed_rows(0)
+    ag_finish(dz, TZ, 2)
     rs_forward(R3, 0)
     ag_forward(dz, TZ, 1)
-    ag_finish(dz, TZ, 2)
     widen_back(2)
     ag_finish(dz, TZ, 1)
     grad_tile(GS, 3)
+    normed_rows(2)
+    rs_forward(R3, 2)
     widen_back(1)
+    grad_tile(GE, 3)
     rs_finish(R3, 0)
     norm_first_back(0)
     ag_start(dh, TH, 0)
-    grad_tile(GE, 3)
+    grad_forward(GS, 3)
+    grad_tile(GE, 2)
+    grad_tile(GS, 2)
+    grad_tile(GE, 1)
     normed_rows(1)
+    rs_finish(R3, 2)
+    norm_first_back(2)
+    ag_start(dh, TH, 2)
+    grad_forward(GE, 3)
+    ag_forward(dh, TH, 0)
     rs_forward(R3, 1)
-    grad_forward(GS, 3)
-    grad_tile(GS, 2)
-    normed_rows(2)
-    ag_forward(dh, TH, 0)
-    rs_forward(R3, 2)
-    grad_forward(GE, 3)
-    grad_tile(GE, 2)
     ag_finish(dh, TH, 0)
     attention_back(0)
+    grad_forward(GE, 2)
+    token_rows(0)
+    ag_forward(dh, TH, 2)
+    grad_tile(GS, 1)
+    grad_forward(GS, 2)
     rs_finish(R3, 1)
     norm_first_back(1)
     ag_start(dh, TH, 1)
-    grad_forward(GS, 2)
-    grad_tile(GS, 1)
-    grad_forward(GE, 2)
-    rs_finish(R3, 2)
-    norm_first_back(2)
-    ag_start(dh, TH, 2)
-    rows_in(MIX, 0, n_seq, out_mixed)
-    grad_tile(GE, 1)
-    token_rows(0)
+    ag_finish(dh, TH, 2)
+    attention_back(2)
+    grad_forward(GE, 1)
+    grad_tile(GE, 0)
     ag_forward(dh, TH, 1)
     grad_forward(GS, 1)
-    grad_tile(GS, 0)
     rs_forward(R4, 0)
-    ag_forward(dh, TH, 2)
     ag_finish(dh, TH, 1)
-    grad_forward(GE, 1)
-    ag_finish(dh, TH, 2)
+    rows_in(MIX, 0, n_seq, out_mixed)
     grad_tile(GO, 3)
-    attention_back(2)
+    grad_tile(GO, 2)
+    attention_back(1)
+    grad_forward(GO, 3)
+    grad_tile(G3, 3)
+    grad_forward(GE, 0)
     rs_finish(R4, 0)
     finish_rows(0)
     rows_out(BACK, 0, 1, back_send, back_recv)
-    grad_forward(GO, 3)
-    grad_tile(GO, 2)
-    attention_back(1)
-    grad_tile(G3, 3)
+    token_rows(2)
+    rs_forward(R4, 2)
+    grad_tile(G3, 2)
+    small_start()
+    grad_tile(GO, 1)
+    grad_forward(G3, 3)
     token_rows(1)
+    grad_tile(G3, 1)
     grad_forward(GO, 2)
-    small_start()
+    rs_finish(R4, 2)
+    finish_rows(2)
+    rows_out(BACK, 2, 1, back_send, back_recv)
+    grad_forward(G3, 2)
+    grad_tile(G3, 0)
+    grad_tile(GS, 0)
+    rows_in(BACK, 0, 1, back_recv)
     rs_forward(R4, 1)
-    grad_tile(GO, 1)
-    grad_tile(G3, 2)
-    grad_forward(G3, 3)
-    token_rows(2)
-    grad_tile(G3, 1)
+    small_forward()
     grad_forward(GO, 1)
+    grad_tile(GO, 0)
     rs_finish(R4, 1)
     finish_rows(1)
     rows_out(BACK, 1, 1, back_send, back_recv)
-    grad_forward(G3, 2)
-    grad_tile(GE, 0)
-    rows_in(BACK, 0, 1, back_recv)
-    rs_forward(R4, 2)
-    small_forward()
-    grad_tile(GO, 0)
-    grad_tile(G3, 0)
-    rs_finish(R4, 2)
-    finish_rows(2)
-    rows_out(BACK, 2, 1, back_send, back_recv)
+    small_finish()
+    grad_forward(G3, 1)
+    rows_in(BACK, 2, 1, back_recv)
+    grad_forward(GO, 0)
     grad_forward(GS, 0)
-    grad_forward(G3, 1)
-    grad_forward(GO, 0)
-    small_finish()
-    grad_forward(GE, 0)
+    grad_forward(G3, 0)
     rows_in(BACK, 1, 1, back_recv)
-    grad_forward(G3, 0)
-    rows_in(BACK, 2, 1, back_recv)
     link.drain()
 
 

time: 224 us -> 221 us (0.987)
  Pallas kernels: 224 us -> 221 us
    pallas_call x1, Pallas kernels: 220 us -> 217 us  [body(): pl.pallas_call(functools.partial(layer_kernel, g), out_shape=(sds(tokens....]
where the time goes in v5:
time: 221 us
  Pallas kernels  221 us (100%)
    pallas_call x1, Pallas kernels, body(): pl.pallas_call(functools.partial(layer_kernel, g), out_shape=(sds(tokens....  217 us

profile of v5, /device:TPU:0, one launch (start us, length us, event | category | flops | bytes accessed | tf_op | source)
XLA Modules:
  0.0 221.3 jit_solution(14990017543982223188)
XLA Ops:
  0.6 217.0 %shard_map.178 = (bf16[24,16,1024]{2,1,0:T(8,128)(2,1)}, bf16[24,16,1024]{2,1,0:T(8,128)(2,1)}, f32[128,768]{1,0:T(8,128)}, f32[128,256]{1,0:T(8,128)}, f32[128,...) custom-call(s32[24]{0:T(128)} %order_s.1, s32[24]{0:T(128)} %refs_1_.1, bf16[24,16,1024]{2,1,0:T(8,128)(2,1)} %bitcast.10, ...), custom_call_target="tpu_custom_call" | custom-call | flops 31809601536 | bytes 16777216 | tf_op jit(solution)/shard_map/pallas_call | solution.py:1326
  217.6 3.7 %shard_map.179 = (bf16[24,16,1024]{2,1,0:T(8,128)(2,1)}, bf16[24,16,1024]{2,1,0:T(8,128)(2,1)}, f32[3,128,256]{2,1,0:T(8,128)}, f32[256,128]{1,0:T(8,128)}, f32[...) custom-call(s32[24]{0:T(128)} %order_s.1, ...), custom_call_target="tpu_custom_call" | custom-call | tf_op jit(solution)/shard_map/pallas_call | solution.py:1359
